TPU v7x, 32 devices: a whole 2x2x4 slice. The times are simulated.
32 devices in a mesh: band: 8 (over z, y), patch: 4 (over x, core).
Axes of the slice: x: 2, y: 2, z: 4, core: 2. Of those that a mesh axis runs over, the one named last changes fastest.
Arguments:
- grid_state: bfloat16 [32, 1024, 512], P('band', 'patch'), may hold values from -6 to 6
- mesh_state: bfloat16 [8, 4, 256, 512], P('band', 'patch'), may hold values from -6 to 6
- g2m_features: bfloat16 [8, 4, 2048, 512], P('band', 'patch'), may hold values from -6 to 6
- g2m_sender: int32 [8, 4, 2048], P('band', 'patch'), may hold values from 0 to 2079, as said below
- g2m_receiver: int32 [8, 4, 2048], P('band', 'patch'), may hold values from 0 to 255
- g2m_blocks: int32 [8, 4], replicated, may hold values from 4 to 16, as said below
- proc_features: bfloat16 [8, 4, 2048, 512], P('band', 'patch'), may hold values from -6 to 6
- proc_sender: int32 [8, 4, 2048], P('band', 'patch'), may hold values from 0 to 2815, as said below
- proc_receiver: int32 [8, 4, 2048], P('band', 'patch'), may hold values from 0 to 255
- dec_features: bfloat16 [3, 32, 1024, 512], P(None, 'band', 'patch'), may hold values from -6 to 6
- dec_sender: int32 [3, 32, 1024], P(None, 'band', 'patch'), may hold values from 0 to 2111, as said below
- enc_weights: bfloat16 [9, 512, 512], replicated, may hold values from -0.25 to 0.25
- proc_weights: bfloat16 [7, 512, 512], replicated, may hold values from -0.25 to 0.25
- dec_weights: bfloat16 [7, 512, 512], replicated, may hold values from -0.25 to 0.25
Outputs:
- grid_out: bfloat16 [32, 1024, 512], P('band', 'patch')
Inputs may be any that keep to these rules, and one draw needn't show every extreme that they name: `g2m_blocks`: the bands at both poles hold 16 live blocks in every sector. `g2m_sender`: never a latitude row before the first or after the last of the grid. `proc_sender`: below 2304, s % 256 is below 64 unless s // 256 = 4; never a band before the first or after the last. `dec_sender`: s % 256 is below 64 unless s // 256 = 4; never a band before the first or after the last.
All inputs are finite; a program needn't handle non-finite values.
Results may differ from a plain program's by a relative error of at most 0.0095.
Values may be sent and summed in bfloat16 or wider, within the bound.
A program may use at most 128 MiB of HBM per device.

v0:
```python
import jax
import jax.numpy as jnp
from jax import lax
from jax.sharding import PartitionSpec as P

COARSE_DEV = 16
HALO = 2


epsilon = 1e-05


def padded_2(cells, sides, width):
    for axis, dim in sides:
        count = lax.axis_size(axis)
        head = lax.slice_in_dim(cells, 0, width, axis=dim)
        tail = lax.slice_in_dim(cells, cells.shape[dim] - width, cells.shape[dim], axis=dim)
        cells = jnp.concatenate(
            [
                lax.ppermute(tail, axis, [(i, (i + 1) % count) for i in range(count)]),
                cells,
                lax.ppermute(head, axis, [((i + 1) % count, i) for i in range(count)]),
            ],
            axis=dim,
        )
    return cells


def layer_norm(values):
    average = jnp.mean(values, axis=-1, keepdims=True)
    centred = values - average
    spread = jnp.mean(centred * centred, axis=-1, keepdims=True)
    return centred * lax.rsqrt(spread + epsilon)


def project(values, weight):
    return jnp.dot(values, weight, preferred_element_type=jnp.float32)


def edge_message(features, send_rows, recv_rows, w_edge, w_out):
    before = (
        project(features, w_edge) + send_rows.astype(jnp.float32) + recv_rows.astype(jnp.float32)
    )
    hidden = jax.nn.silu(before).astype(jnp.bfloat16)
    return layer_norm(project(hidden, w_out)).astype(jnp.bfloat16)


def node_update(current, summed, w_self, w_total, w_out):
    before = project(current, w_self) + project(summed.astype(jnp.bfloat16), w_total)
    hidden = jax.nn.silu(before).astype(jnp.bfloat16)
    return (current.astype(jnp.float32) + layer_norm(project(hidden, w_out))).astype(jnp.bfloat16)


def self_update(current, w_first, w_out):
    hidden = jax.nn.silu(project(current, w_first)).astype(jnp.bfloat16)
    return (current.astype(jnp.float32) + layer_norm(project(hidden, w_out))).astype(jnp.bfloat16)


def one_hot_sum(summed, message, receiver):
    matches = (
        lax.broadcasted_iota(jnp.int32, (summed.shape[0], receiver.shape[0]), 0)
        == receiver[None, :]
    )
    return summed + jnp.dot(
        matches.astype(jnp.bfloat16), message, preferred_element_type=jnp.float32
    )


def shards(
    grid_state,
    mesh_state,
    g2m_features,
    g2m_sender,
    g2m_receiver,
    g2m_blocks,
    proc_features,
    proc_sender,
    proc_receiver,
    dec_features,
    dec_sender,
    enc_weights,
    proc_weights,
    dec_weights,
):
    lat_rows, lon_cols, latent = grid_state.shape
    node_count = mesh_state.shape[2]
    cell_count = lat_rows * lon_cols
    grid_flat = grid_state.reshape(cell_count, latent)
    mesh_flat = mesh_state.reshape(node_count, latent)
    grid_send = (
        project(grid_flat, enc_weights[0]).astype(jnp.bfloat16).reshape(lat_rows, lon_cols, latent)
    )
    padded = padded_2(grid_send, (("band", 0), ("patch", 1)), HALO)
    send_table = padded.reshape(-1, latent)
    mesh_recv = project(mesh_flat, enc_weights[1]).astype(jnp.bfloat16)
    enc_feats = g2m_features.reshape(-1, latent)
    enc_senders = g2m_sender.reshape(-1)
    enc_receivers = g2m_receiver.reshape(-1)
    band_index = lax.axis_index("band")
    patch_index = lax.axis_index("patch")
    own_blocks = g2m_blocks[band_index, patch_index]
    w_edge = enc_weights[2]
    w_out = enc_weights[3]

    def own_step(block, summed):
        start = block * 128
        features = lax.dynamic_slice_in_dim(enc_feats, start, 128, 0)
        sender = lax.dynamic_slice_in_dim(enc_senders, start, 128, 0)
        receiver = lax.dynamic_slice_in_dim(enc_receivers, start, 128, 0)
        send_rows = jnp.take(send_table, sender, axis=0)
        recv_rows = jnp.take(mesh_recv, receiver, axis=0)
        return one_hot_sum(
            summed, edge_message(features, send_rows, recv_rows, w_edge, w_out), receiver
        )

    empty = jnp.zeros((node_count, latent), jnp.float32)
    summed = lax.fori_loop(0, own_blocks, own_step, empty)
    mesh_next = node_update(mesh_flat, summed, enc_weights[4], enc_weights[5], enc_weights[6])
    grid_next = self_update(grid_flat, enc_weights[7], enc_weights[8])
    proc_send = project(mesh_next, proc_weights[0]).astype(jnp.bfloat16)
    proc_recv = project(mesh_next, proc_weights[1]).astype(jnp.bfloat16)
    coarse_all = lax.all_gather(
        proc_send[node_count - COARSE_DEV :], ("band", "patch"), axis=0, tiled=True
    )
    proc_senders = proc_sender.reshape(-1)
    rim_rows = padded_2(proc_send.reshape(1, 1, node_count, latent), (("band", 0), ("patch", 1)), 1)
    source = jnp.concatenate([rim_rows.reshape(-1, latent), coarse_all], axis=0)
    proc_receivers = proc_receiver.reshape(-1)
    message = edge_message(
        proc_features.reshape(-1, latent),
        jnp.take(source, proc_senders, axis=0),
        jnp.take(proc_recv, proc_receivers, axis=0),
        proc_weights[2],
        proc_weights[3],
    )
    proc_total = one_hot_sum(empty, message, proc_receivers)
    mesh_last = node_update(
        mesh_next, proc_total, proc_weights[4], proc_weights[5], proc_weights[6]
    )
    dec_send = project(mesh_last, dec_weights[0]).astype(jnp.bfloat16)
    dec_senders = dec_sender.reshape(-1)
    dec_rows = padded_2(dec_send.reshape(1, 1, node_count, latent), (("band", 0), ("patch", 1)), 1)
    dec_source = dec_rows.reshape(-1, latent)
    dec_recv = project(grid_next, dec_weights[1]).astype(jnp.bfloat16)
    before = project(dec_features.reshape(-1, latent), dec_weights[2]).reshape(
        3, cell_count, latent
    )
    before = before + jnp.take(dec_source, dec_senders, axis=0).astype(jnp.float32).reshape(
        3, cell_count, latent
    )
    before = before + dec_recv.astype(jnp.float32)[None]
    hidden = jax.nn.silu(before).astype(jnp.bfloat16).reshape(-1, latent)
    dec_message = (
        layer_norm(project(hidden, dec_weights[3]))
        .astype(jnp.bfloat16)
        .reshape(3, cell_count, latent)
    )
    dec_total = jnp.sum(dec_message.astype(jnp.float32), axis=0)
    result = node_update(grid_next, dec_total, dec_weights[4], dec_weights[5], dec_weights[6])
    return result.reshape(lat_rows, lon_cols, latent)


def solution(mesh):
    placed = (
        P("band", "patch", None),
        P("band", "patch", None, None),
        P("band", "patch", None, None),
        P("band", "patch", None),
        P("band", "patch", None),
        P(),
        P("band", "patch", None, None),
        P("band", "patch", None),
        P("band", "patch", None),
        P(None, "band", "patch", None),
        P(None, "band", "patch"),
        P(),
        P(),
        P(),
    )
    return jax.shard_map(
        shards, mesh=mesh, in_specs=placed, out_specs=P("band", "patch", None), check_vma=False
    )
```

profile of v0, /device:TPU:0, one launch (start us, length us, event | category | flops | bytes accessed | tf_op | source)
XLA Modules:
  0.0 428.7 jit_solution(1145235535695072667)
XLA Ops:
  4.3 3.0 collective-permute-start
  7.2 3.0 collective-permute-start.1
  12.6 4.3 fusion.117
  21.9 3.6 fusion.26
  37.5 3.1 pad_maximum_fusion.3
  40.5 4.0 reshape.277
  45.3 195.0 %while.10 = (s32[]{:T(128)}, f32[256,512]{1,0:T(8,128)}, s32[]{:T(128)}, s32[2048]{0:T(1024)}, bf16[2048,512]{1,0:T(8,128)(2,1)}, /*index=5*/bf16[512,512]{1,0:T...) while((s32[]{:T(128)}, f32[256,512]{1,0:T(8,128)}, ...), condition=%wide.region_5.6_spmd, body=%wide.region_2.5_spmd.sunk | while | flops 169119744 | bytes 3820603 | solution.py:117
  48.3 3.4 gather_fusion.1
  51.7 2.4 fusion.155
  60.4 3.4 gather_fusion.1
  72.6 3.4 gather_fusion.1
  84.7 3.4 gather_fusion.1
  88.1 2.4 fusion.155
  96.9 3.4 gather_fusion.1
  109.0 3.4 gather_fusion.1
  121.2 3.4 gather_fusion.1
  133.3 3.4 gather_fusion.1
  145.4 3.4 gather_fusion.1
  157.6 3.4 gather_fusion.1
  169.7 3.4 gather_fusion.1
  181.9 3.4 gather_fusion.1
  194.0 3.4 gather_fusion.1
  206.2 3.4 gather_fusion.1
  218.3 3.4 gather_fusion.1
  230.4 3.4 gather_fusion.1
  240.4 2.9 fusion.120
  247.3 4.7 %collective-permute-start.5 = (bf16[1,1,256,512]{3,2,1,0:T(8,128)(2,1)S(1)}, bf16[1,1,256,512]{3,2,1,0:T(8,128)(2,1)S(1)}, u32[]{:S(2)}, u32[]{:S(2)}) collective-permute-start(bf16[1,1,256,512]{3,2,1,0:T(8,128)(2,1)S(1)} %bitcast.169), channel_id=1, source_target_pairs={{4,0},{8,4},{12,8},{16,12},{20,16},{24,20},{28,24},{0,28},{5,1},{9... | collective-permute-start | bytes 786440 | tf_op jit(solution)/shard_map/ppermute | solution.py:22
  252.1 6.6 %collective-permute-done.4 = bf16[1,1,256,512]{3,2,1,0:T(8,128)(2,1)S(1)} collective-permute-done((bf16[1,1,256,512]{3,2,1,0:T(8,128)(2,1)S(1)}, bf16[1,1,256,512]{3,2,1,0:T(8,128)(2,1)S(1)}, u32[]{:S(2)}, u32[]{:S(2)}) %collective-permute-start.4) | collective-permute-done | bytes 262176 | tf_op jit(solution)/shard_map/ppermute | solution.py:20
  258.6 2.9 collective-permute-done.5
  265.7 9.2 %gather_fusion.3 = bf16[2048,512]{1,0:T(8,128)(2,1)} fusion(bf16[256,512]{1,0:T(8,128)(2,1)S(1)} %convolution_convert_fusion.3, s32[2048]{0:T(1024)S(1)} %broadcast_clamp_fusion.1), kind=kCustom, calls=%fused_computation.3 | custom fusion | bytes 4202496 | tf_op jit(solution)/shard_map/jit(_take)/gather | solution.py:132
  274.9 41.3 %all_gather.3 = bf16[512,512]{1,0:T(8,128)(2,1)S(1)} all-gather(bf16[16,512]{1,0:T(8,128)(2,1)S(1)} %slice.132), channel_id=1, replica_groups=mesh['band'=8,'patch'=4] {'band','patch'}, dimensions={0}, use_global_device_ids=true | all-gather | bytes 540672 | tf_op jit(solution)/shard_map/all_gather | solution.py:122
  321.9 11.4 %gather_fusion.2 = bf16[2048,512]{1,0:T(8,128)(2,1)} fusion(bf16[2816,512]{1,0:T(8,128)(2,1)} %pad_maximum_fusion, s32[2048]{0:T(1024)S(1)} %broadcast_clamp_fusion.2), kind=kCustom, calls=%fused_computation.2 | custom fusion | bytes 4202496 | tf_op jit(solution)/shard_map/jit(_take)/gather | solution.py:131
  333.4 7.2 %fusion.125 = (f32[2048]{0:T(1024)S(1)}, f32[2048,512]{0,1:T(8,128)}) fusion(bf16[7,512,512]{2,1,0:T(8,128)(2,1)} %param.28, bf16[1,1,2048,512]{3,2,1,0:T(8,128)(2,1)} %param.22, bf16[2048,512]{1,0:T(8,128)(2,1)} %gather_fusion.3, bf16[2048,512]{1,0:T(8,128)(2,1)} %gather_fusion.2, pred[2048]{0:T(1024)(128)(4,1)S(1)} %get-tuple-element.105, ...), kind=kOutput, calls=%fused_computation.176 | convolution fusion | flops 2160064512 | bytes 11546624 | tf_op jit(solution)/shard_map/dot_general | solution.py:37
  340.6 2.6 multiply_reduce_fusion.2
  343.3 4.4 %multiply_convert_fusion.15 = bf16[256,512]{1,0:T(8,128)(2,1)} fusion(f32[256,512]{1,0:T(8,128)} %fusion.50, f32[2048,512]{0,1:T(8,128)} %get-tuple-element.98, f32[2048]{0:T(1024)S(1)} %add_rsqrt_fusion.2, f32[2048]{0:T(1024)S(1)} %broadcast_multiply_fusion.2, s32[2048]{0:T(1024)S(1)} %bitcast.179, bf16[7,512,512]{2,1,0:T(8,128)(2,1)} %param.28), kind=kOutput, calls=%fused_computation.113 | convolution fusion | flops 675676160 | bytes 5529600 | tf_op jit(solution)/shard_map/dot_general | solution.py:37
  351.0 4.7 %collective-permute-start.9 = (bf16[1,1,256,512]{3,2,1,0:T(8,128)(2,1)S(1)}, bf16[1,1,256,512]{3,2,1,0:T(8,128)(2,1)S(1)}, u32[]{:S(2)}, u32[]{:S(2)}) collective-permute-start(bf16[1,1,256,512]{3,2,1,0:T(8,128)(2,1)S(1)} %fusion.29), channel_id=1, source_target_pairs={{4,0},{8,4},{12,8},{16,12},{20,16},{24,20},{28,24},{0,28},{5,1},{9... | collective-permute-start | bytes 786440 | tf_op jit(solution)/shard_map/ppermute | solution.py:22
  355.7 6.6 %collective-permute-done.8 = bf16[1,1,256,512]{3,2,1,0:T(8,128)(2,1)S(1)} collective-permute-done((bf16[1,1,256,512]{3,2,1,0:T(8,128)(2,1)S(1)}, bf16[1,1,256,512]{3,2,1,0:T(8,128)(2,1)S(1)}, u32[]{:S(2)}, u32[]{:S(2)}) %collective-permute-start.8) | collective-permute-done | bytes 262176 | tf_op jit(solution)/shard_map/ppermute | solution.py:20
  362.3 2.9 collective-permute-done.9
  367.1 3.0 fusion.61
  370.1 5.5 %fusion.59 = f32[3,1024,512]{2,1,0:T(8,128)} fusion(bf16[3,1024,512]{2,1,0:T(8,128)(2,1)S(1)} %bitcast.160, bf16[7,512,512]{2,1,0:T(8,128)(2,1)} %param.29), kind=kOutput, calls=%fused_computation.98 | convolution fusion | flops 1610612736 | bytes 9961472 | tf_op jit(solution)/shard_map/dot_general | solution.py:37
  375.6 9.5 %collective-permute-done.10 = bf16[3,1,256,512]{3,2,1,0:T(8,128)(2,1)S(1)} collective-permute-done((bf16[3,1,256,512]{3,2,1,0:T(8,128)(2,1)S(1)}, bf16[3,1,256,512]{3,2,1,0:T(8,128)(2,1)S(1)}, u32[]{:S(2)}, u32[]{:S(2)}) %collective-permute-start.10) | collective-permute-done | bytes 786464 | tf_op jit(solution)/shard_map/ppermute | solution.py:20
  386.7 15.3 %gather_fusion.4 = bf16[3072,512]{1,0:T(8,128)(2,1)} fusion(bf16[2304,512]{1,0:T(8,128)(2,1)} %bitcast.161, s32[3072]{0:T(1024)S(1)} %broadcast_clamp_fusion), kind=kCustom, calls=%fused_computation.4 | custom fusion | bytes 6303744 | tf_op jit(solution)/shard_map/jit(_take)/gather | solution.py:148
  402.0 5.4 %multiply_convert_fusion.4 = bf16[3,1024,512]{2,1,0:T(8,128)(2,1)S(1)} fusion(f32[3,1024,512]{2,1,0:T(8,128)} %fusion.59, f32[1024,512]{1,0:T(8,128)} %fusion.26, bf16[3,1024,512]{2,1,0:T(8,128)(2,1)} %bitcast.164, pred[3,1024]{1,0:T(4,128)(4,1)S(1)} %compare_and_fusion.2), kind=kLoop, calls=%fused_computation.38 | loop fusion | flops 14155776 | bytes 14683136 | tf_op jit(solution)/shard_map/convert_element_type | solution.py:152
  407.4 2.9 fusion.131
  412.5 2.8 multiply_convert_fusion.3
  415.3 3.7 reduce_sum.148
  419.0 4.9 %fusion.132 = (f32[1024]{0:T(1024)S(1)}, f32[1024,512]{1,0:T(8,128)}) fusion(bf16[7,512,512]{2,1,0:T(8,128)(2,1)} %param.29, f32[1024,512]{1,0:T(8,128)} %fusion.61, bf16[1024,512]{1,0:T(8,128)(2,1)} %reduce_sum.148), kind=kOutput, calls=%fused_computation.179 | convolution fusion | flops 1077410816 | bytes 6295552 | tf_op jit(solution)/shard_map/dot_general | solution.py:37
  426.1 2.6 add_convert_fusion
  (267 shorter events, 172.7 us)
Async XLA Ops:
  0.0 370.1 %copy-start = (bf16[3,4,256,512]{3,2,1,0:T(8,128)(2,1)S(1)}, bf16[3,4,256,512]{3,2,1,0:T(8,128)(2,1)}, u32[]{:S(2)}) copy-start(bf16[3,4,256,512]{3,2,1,0:T(8,128)(2,1)} %param.25) | copy-start | bytes 9437188
  2.2 1.0 copy-start.3
  4.3 25.7 %collective-permute-start = (bf16[2,256,512]{2,1,0:T(8,128)(2,1)}, bf16[2,256,512]{2,1,0:T(8,128)(2,1)}, u32[]{:S(2)}, u32[]{:S(2)}) collective-permute-start(bf16[2,256,512]{2,1,0:T(8,128)(2,1)} %bitcast.15), channel_id=1, source_target_pairs={{0,4},{4,8},{8,12},{12,16},{16,20},{20,24},{24,28},{28,0},{1,5},{5... | collective-permute-start | bytes 1572872 | tf_op jit(solution)/shard_map/ppermute | solution.py:20
  7.2 24.9 %collective-permute-start.1 = (bf16[2,256,512]{2,1,0:T(8,128)(2,1)}, bf16[2,256,512]{2,1,0:T(8,128)(2,1)}, u32[]{:S(2)}, u32[]{:S(2)}) collective-permute-start(bf16[2,256,512]{2,1,0:T(8,128)(2,1)} %bitcast.17), channel_id=1, source_target_pairs={{4,0},{8,4},{12,8},{16,12},{20,16},{24,20},{28,24},{0,28},{5,1},{9... | collective-permute-start | bytes 1572872 | tf_op jit(solution)/shard_map/ppermute | solution.py:22
  12.6 4.3 copy-start.17
  12.6 4.9 %copy-start.14 = (s32[3,4,256]{2,1,0:T(4,128)S(1)}, s32[3,4,256]{2,1,0:T(4,128)}, u32[]{:S(2)}) copy-start(s32[3,4,256]{2,1,0:T(4,128)} %param.26) | copy-start | bytes 36868
  17.5 2.7 copy-start.5
  20.1 5.3 %copy-start.10 = (bf16[1,1,256,512]{3,2,1,0:T(8,128)(2,1)S(1)}, bf16[1,1,256,512]{3,2,1,0:T(8,128)(2,1)}, u32[]{:S(2)}) copy-start(bf16[1,1,256,512]{3,2,1,0:T(8,128)(2,1)} %param.17) | copy-start | bytes 786436
  21.9 11.1 %copy-start.1 = (bf16[1024,512]{1,0:T(8,128)(2,1)}, bf16[1024,512]{1,0:T(8,128)(2,1)S(1)}, u32[]{:S(2)}) copy-start(bf16[1024,512]{1,0:T(8,128)(2,1)S(1)} %add_convert_fusion.1) | copy-start | bytes 3145732
  21.9 5.8 %copy-start.19 = (s32[1,1,2048]{2,1,0:T(1,128)S(1)}, s32[1,1,2048]{2,1,0:T(1,128)}, u32[]{:S(2)}) copy-start(s32[1,1,2048]{2,1,0:T(1,128)} %param.24) | copy-start | bytes 24580
  21.9 10.3 %copy-start.4 = (bf16[1024,512]{1,0:T(8,128)(2,1)S(1)}, bf16[1024,512]{1,0:T(8,128)(2,1)}, u32[]{:S(2)}) copy-start(bf16[1024,512]{1,0:T(8,128)(2,1)} %copy-done.3) | copy-start | bytes 3145732
  33.0 4.5 %collective-permute-start.2 = (bf16[8,2,512]{2,1,0:T(2,128)(2,1)S(1)}, bf16[8,2,512]{2,1,0:T(2,128)(2,1)S(1)}, u32[]{:S(2)}, u32[]{:S(2)}) collective-permute-start(bf16[8,2,512]{2,1,0:T(2,128)(2,1)S(1)} %get-tuple-element.89), channel_id=1, source_target_pairs={{0,1},{1,2},{2,3},{3,0},{4,5},{5,6},{6,7},{7,4},{8,9},{9,10},{10,1... | collective-permute-start | bytes 49160 | tf_op jit(solution)/shard_map/ppermute | solution.py:20
  33.0 4.4 %collective-permute-start.3 = (bf16[8,2,512]{2,1,0:T(2,128)(2,1)S(1)}, bf16[8,2,512]{2,1,0:T(2,128)(2,1)S(1)}, u32[]{:S(2)}, u32[]{:S(2)}) collective-permute-start(bf16[8,2,512]{2,1,0:T(2,128)(2,1)S(1)} %get-tuple-element.90), channel_id=1, source_target_pairs={{1,0},{2,1},{3,2},{0,3},{5,4},{6,5},{7,6},{4,7},{9,8},{10,9},{11,1... | collective-permute-start | bytes 49160 | tf_op jit(solution)/shard_map/ppermute | solution.py:22
  240.3 4.3 copy-start.11
  240.3 11.7 %copy-start.22 = (s32[2048,1]{0,1:T(1,128)S(1)}, s32[2048,1]{0,1:T(1,128)}, u32[]{:S(2)}) copy-start(s32[2048,1]{0,1:T(1,128)} %compare_select_fusion.4) | copy-start | bytes 24580
  240.4 11.7 %copy-start.18 = (s32[1,1,2048]{2,1,0:T(1,128)S(1)}, s32[1,1,2048]{2,1,0:T(1,128)}, u32[]{:S(2)}) copy-start(s32[1,1,2048]{2,1,0:T(1,128)} %param.23) | copy-start | bytes 24580
  240.4 11.7 %copy-start.20 = (s32[1,1,2048]{2,1,0:T(1,128)S(1)}, s32[1,1,2048]{2,1,0:T(1,128)}, u32[]{:S(2)}) copy-start(s32[1,1,2048]{2,1,0:T(1,128)} %param.24) | copy-start | bytes 24580
  243.3 21.0 %copy-start.21 = (s32[2048,1]{0,1:T(1,128)S(1)}, s32[2048,1]{0,1:T(1,128)}, u32[]{:S(2)}) copy-start(s32[2048,1]{0,1:T(1,128)} %compare_select_fusion.3) | copy-start | bytes 24580
  243.3 21.0 %copy-start.15 = (s32[3,4,256]{2,1,0:T(4,128)S(1)}, s32[3,4,256]{2,1,0:T(4,128)}, u32[]{:S(2)}) copy-start(s32[3,4,256]{2,1,0:T(4,128)} %param.26) | copy-start | bytes 36868
  245.8 18.5 %copy-start.7 = (bf16[256,512]{1,0:T(8,128)(2,1)}, bf16[256,512]{1,0:T(8,128)(2,1)S(1)}, u32[]{:S(2)}) copy-start(bf16[256,512]{1,0:T(8,128)(2,1)S(1)} %add_convert_fusion.3) | copy-start | bytes 786436
  247.3 17.0 %copy-start.9 = (bf16[256,512]{1,0:T(8,128)(2,1)}, bf16[256,512]{1,0:T(8,128)(2,1)S(1)}, u32[]{:S(2)}) copy-start(bf16[256,512]{1,0:T(8,128)(2,1)S(1)} %convolution_convert_fusion.4) | copy-start | bytes 786436
  247.3 11.4 %collective-permute-start.4 = (bf16[1,1,256,512]{3,2,1,0:T(8,128)(2,1)S(1)}, bf16[1,1,256,512]{3,2,1,0:T(8,128)(2,1)S(1)}, u32[]{:S(2)}, u32[]{:S(2)}) collective-permute-start(bf16[1,1,256,512]{3,2,1,0:T(8,128)(2,1)S(1)} %bitcast.168), channel_id=1, source_target_pairs={{0,4},{4,8},{8,12},{12,16},{16,20},{20,24},{24,28},{28,0},{1,5},{5... | collective-permute-start | bytes 786440 | tf_op jit(solution)/shard_map/ppermute | solution.py:20
  247.3 14.2 %collective-permute-start.5 = (bf16[1,1,256,512]{3,2,1,0:T(8,128)(2,1)S(1)}, bf16[1,1,256,512]{3,2,1,0:T(8,128)(2,1)S(1)}, u32[]{:S(2)}, u32[]{:S(2)}) collective-permute-start(bf16[1,1,256,512]{3,2,1,0:T(8,128)(2,1)S(1)} %bitcast.169), channel_id=1, source_target_pairs={{4,0},{8,4},{12,8},{16,12},{20,16},{24,20},{28,24},{0,28},{5,1},{9... | collective-permute-start | bytes 786440 | tf_op jit(solution)/shard_map/ppermute | solution.py:22
  258.6 5.7 %copy-start.12 = (bf16[1,1,256,512]{3,2,1,0:T(8,128)(2,1)}, bf16[1,1,256,512]{3,2,1,0:T(8,128)(2,1)S(1)}, u32[]{:S(2)}) copy-start(bf16[1,1,256,512]{3,2,1,0:T(8,128)(2,1)S(1)} %collective-permute-done.4) | copy-start | bytes 786436
  261.5 2.8 copy-start.13
  262.5 55.9 %collective-permute-start.6 = (bf16[3,1,256,512]{3,2,1,0:T(8,128)(2,1)}, bf16[3,1,256,512]{3,2,1,0:T(8,128)(2,1)}, u32[]{:S(2)}, u32[]{:S(2)}) collective-permute-start(bf16[3,1,256,512]{3,2,1,0:T(8,128)(2,1)} %pad_maximum_fusion.4), channel_id=1, source_target_pairs={{0,1},{1,2},{2,3},{3,0},{4,5},{5,6},{6,7},{7,4},{8,9},{9,10},{10,1... | collective-permute-start | bytes 2359304 | tf_op jit(solution)/shard_map/ppermute | solution.py:20
  262.5 55.9 %collective-permute-start.7 = (bf16[3,1,256,512]{3,2,1,0:T(8,128)(2,1)}, bf16[3,1,256,512]{3,2,1,0:T(8,128)(2,1)}, u32[]{:S(2)}, u32[]{:S(2)}) collective-permute-start(bf16[3,1,256,512]{3,2,1,0:T(8,128)(2,1)} %pad_maximum_fusion.4), channel_id=1, source_target_pairs={{1,0},{2,1},{3,2},{0,3},{5,4},{6,5},{7,6},{4,7},{9,8},{10,9},{11,1... | collective-permute-start | bytes 2359304 | tf_op jit(solution)/shard_map/ppermute | solution.py:22
  343.3 6.2 %copy-start.8 = (bf16[256,512]{1,0:T(8,128)(2,1)S(1)}, bf16[256,512]{1,0:T(8,128)(2,1)}, u32[]{:S(2)}) copy-start(bf16[256,512]{1,0:T(8,128)(2,1)} %copy-done.7) | copy-start | bytes 786436
  347.7 8.0 %copy-start.16 = (s32[3072,1]{0,1:T(1,128)S(1)}, s32[3072,1]{0,1:T(1,128)}, u32[]{:S(2)}) copy-start(s32[3072,1]{0,1:T(1,128)} %compare_select_fusion.2) | copy-start | bytes 36868
  347.7 19.4 %copy-start.2 = (bf16[1024,512]{1,0:T(8,128)(2,1)S(1)}, bf16[1024,512]{1,0:T(8,128)(2,1)}, u32[]{:S(2)}) copy-start(bf16[1024,512]{1,0:T(8,128)(2,1)} %copy-done.1) | copy-start | bytes 3145732
  350.9 11.4 %collective-permute-start.8 = (bf16[1,1,256,512]{3,2,1,0:T(8,128)(2,1)S(1)}, bf16[1,1,256,512]{3,2,1,0:T(8,128)(2,1)S(1)}, u32[]{:S(2)}, u32[]{:S(2)}) collective-permute-start(bf16[1,1,256,512]{3,2,1,0:T(8,128)(2,1)S(1)} %fusion.29), channel_id=1, source_target_pairs={{0,4},{4,8},{8,12},{12,16},{16,20},{20,24},{24,28},{28,0},{1,5},{5... | collective-permute-start | bytes 786440 | tf_op jit(solution)/shard_map/ppermute | solution.py:20
  351.0 14.2 %collective-permute-start.9 = (bf16[1,1,256,512]{3,2,1,0:T(8,128)(2,1)S(1)}, bf16[1,1,256,512]{3,2,1,0:T(8,128)(2,1)S(1)}, u32[]{:S(2)}, u32[]{:S(2)}) collective-permute-start(bf16[1,1,256,512]{3,2,1,0:T(8,128)(2,1)S(1)} %fusion.29), channel_id=1, source_target_pairs={{4,0},{8,4},{12,8},{16,12},{20,16},{24,20},{28,24},{0,28},{5,1},{9... | collective-permute-start | bytes 786440 | tf_op jit(solution)/shard_map/ppermute | solution.py:22
  365.3 19.9 %collective-permute-start.10 = (bf16[3,1,256,512]{3,2,1,0:T(8,128)(2,1)S(1)}, bf16[3,1,256,512]{3,2,1,0:T(8,128)(2,1)S(1)}, u32[]{:S(2)}, u32[]{:S(2)}) collective-permute-start(bf16[3,1,256,512]{3,2,1,0:T(8,128)(2,1)S(1)} %pad_maximum_fusion.5), channel_id=1, source_target_pairs={{0,1},{1,2},{2,3},{3,0},{4,5},{5,6},{6,7},{7,4},{8,9},{9,10},{10,1... | collective-permute-start | bytes 2359304 | tf_op jit(solution)/shard_map/ppermute | solution.py:20
  365.3 19.8 %collective-permute-start.11 = (bf16[3,1,256,512]{3,2,1,0:T(8,128)(2,1)S(1)}, bf16[3,1,256,512]{3,2,1,0:T(8,128)(2,1)S(1)}, u32[]{:S(2)}, u32[]{:S(2)}) collective-permute-start(bf16[3,1,256,512]{3,2,1,0:T(8,128)(2,1)S(1)} %pad_maximum_fusion.5), channel_id=1, source_target_pairs={{1,0},{2,1},{3,2},{0,3},{5,4},{6,5},{7,6},{4,7},{9,8},{10,9},{11,1... | collective-permute-start | bytes 2359304 | tf_op jit(solution)/shard_map/ppermute | solution.py:22
  423.9 2.2 copy-start.6
where the time goes:
time: 432 us; the launch traced here: 429 us
  matrix products  127 us (29%)
  local copies, waits for them, and re-layouts  114 us (26%)
  other arithmetic  80 us (19%)
  blocking collectives  41.3 us (10%)
  waiting for transfers between devices  32.4 us (8%)
  starting transfers between devices  20.9 us (5%)
  loops' own time  12.4 us (3%)
    dot_general x33, matrix products, project(): return jnp.dot(values, weight, preferred_element_type=jnp.float32)  91.3 us
    gather x16, local copies, waits for them, and re-layouts, own_step(): send_rows = jnp.take(send_table, sender, axis=0)  54.3 us
    all_gather x1, blocking collectives, shards(): lax.all_gather(proc_send[node_count - COARSE_DEV:], ('band', 'patch'), ax...  41.3 us
    dot_general x16, matrix products, one_hot_sum(): jnp.dot(matches.astype(jnp.bfloat16), message, preferred_element_type=jnp...  35.6 us
    reduce_sum x22, other arithmetic, layer_norm(): spread = jnp.mean(centred * centred, axis=-1, keepdims=True)  28.3 us
    ppermute x6, waiting for transfers between devices, padded_2(): lax.ppermute(tail, axis, [(i, (i + 1) % count) for i in range(count)])  24.4 us
    and x16, other arithmetic, own_step(): recv_rows = jnp.take(mesh_recv, receiver, axis=0)  21.8 us
    ppermute x6, starting transfers between devices, padded_2(): lax.ppermute(head, axis, [((i + 1) % count, i) for i in range(count)])  17.7 us
  transfers between devices with their start and end apart: 12, of which 7 were waited for; matrix products, arithmetic and copies ran while one was open for 10% of the time, Pallas kernels for 0%

commit v1 on v0

v1 whole, which is shorter than its diff:
```python
import functools

import jax
import jax.numpy as jnp
from jax import lax
from jax.experimental import pallas as pl
from jax.experimental.pallas import tpu as pltpu
from jax.sharding import PartitionSpec as P

MESH = pl.DeviceIdType.MESH
COARSE_DEV = 16
HALO = 2
BORDER = 64
EPSILON = 1e-05
BF = jnp.bfloat16
F32 = jnp.float32
ROWS = 512

G_NORTH, G_SOUTH, G_WEST, G_EAST = 0, 3, 6, 7
G_FORWARD = 8
P_SIDE, P_FORWARD, D_SIDE, D_FORWARD = 12, 16, 20, 24
C_BASE = 28


def dot(a, b):
    return jnp.dot(a, b, preferred_element_type=F32)


def silu(v):
    half = 0.5 * v
    return half + half * jnp.tanh(half)


def layer_norm(v):
    centred = v - jnp.mean(v, axis=-1, keepdims=True)
    spread = jnp.mean(centred * centred, axis=-1, keepdims=True)
    return centred * lax.rsqrt(spread + EPSILON)


def columns_of(row):
    n = row.shape[1]
    wide = jnp.broadcast_to(row.astype(F32), (128, n)).T
    return wide.astype(jnp.int32).astype(jnp.int16)


def pick(columns, first, count):
    lane = lax.broadcasted_iota(jnp.int16, columns.shape, 1)
    parts = []
    for start in range(first, first + count, 128):
        hit = columns == lane + jnp.int16(start)
        parts.append(jnp.where(hit, BF(1), BF(0)))
    return jnp.concatenate(parts, axis=1) if len(parts) > 1 else parts[0]


def scatter(row, nodes):
    hit = lax.broadcasted_iota(jnp.int32, (nodes, row.shape[1]), 0) == row
    return jnp.where(hit, 1.0, 0.0).astype(BF)


def body(
    bands,
    patches,
    grid_in,
    mesh_in,
    gfeat_in,
    gsend_in,
    grecv_in,
    blocks,
    pfeat_in,
    psend_in,
    precv_in,
    dfeat_in,
    dsend_in,
    encw_in,
    procw_in,
    decw_in,
    out,
    grid,
    mesh,
    gfeat,
    gsend,
    grecv,
    pfeat,
    psend,
    precv,
    dfeat,
    dsend,
    encw,
    procw,
    decw,
    table,
    mrecv,
    gnext,
    pre_g,
    pre_p,
    pre_d,
    upd,
    total,
    mnext,
    pown,
    pnear,
    pcoarse,
    precv_rows,
    down,
    dnear,
    result,
    in_sem,
    out_sem,
    send_sem,
    recv_sem,
):
    band, patch = lax.axis_index("band"), lax.axis_index("patch")
    has_north, has_south = band > 0, band < bands - 1
    west, east = lax.rem(patch + patches - 1, patches), lax.rem(patch + 1, patches)
    lat, lon, latent = grid.shape
    nodes = mesh.shape[0]
    half_lat = ROWS // lon

    loads = {}

    def load(name, src, dst):
        copy = pltpu.make_async_copy(src, dst, in_sem.at[len(loads)])
        copy.start()
        loads[name] = copy

    load("grid", grid_in, grid)
    load("e0", encw_in.at[0], encw.at[0])
    load("e78", encw_in.at[pl.ds(7, 2)], encw.at[pl.ds(7, 2)])
    load("mesh", mesh_in.at[0, 0], mesh)
    load("e12", encw_in.at[pl.ds(1, 2)], encw.at[pl.ds(1, 2)])
    load("gs", gsend_in.at[0], gsend)
    load("gr", grecv_in.at[0], grecv)
    load("gf", gfeat_in.at[0, 0], gfeat)
    load("p2", procw_in.at[2], procw.at[2])
    load("pf", pfeat_in.at[0, 0], pfeat)
    load("e36", encw_in.at[pl.ds(3, 4)], encw.at[pl.ds(3, 4)])
    load("p01", procw_in.at[pl.ds(0, 2)], procw.at[pl.ds(0, 2)])
    load("ps", psend_in.at[0], psend)
    load("pr", precv_in.at[0], precv)
    load("d", decw_in, decw)
    load("df", dfeat_in, dfeat)
    load("ds", dsend_in, dsend)
    load("p36", procw_in.at[pl.ds(3, 4)], procw.at[pl.ds(3, 4)])

    def need(*names):
        for name in names:
            loads[name].wait()

    barrier = pltpu.get_barrier_semaphore()
    for k in range(1, bands):
        pl.semaphore_signal(
            barrier, inc=1, device_id={"band": lax.rem(band + k, bands), "patch": patch}, device_id_type=MESH
        )
    greeted = [k for k in range(1, patches) if k in (1, patches - 1) or k % 2 == 0]
    for k in greeted:
        pl.semaphore_signal(
            barrier, inc=1, device_id={"band": band, "patch": lax.rem(patch + k, patches)}, device_id_type=MESH
        )

    def remote(src, dst, number, to_band, to_patch):
        return pltpu.make_async_remote_copy(
            src_ref=src,
            dst_ref=dst,
            send_sem=send_sem.at[number],
            recv_sem=recv_sem.at[number],
            device_id={"band": to_band, "patch": to_patch},
            device_id_type=MESH,
        )

    @pl.when(jnp.logical_not(has_north))
    def _():
        table[4:6] = jnp.zeros_like(table[4:6])
        table[8, 8:12] = jnp.zeros_like(table[8, 8:12])
        pnear[0:3] = jnp.zeros_like(pnear[0:3])
        dnear[0:3] = jnp.zeros_like(dnear[0:3])

    @pl.when(jnp.logical_not(has_south))
    def _():
        table[6:8] = jnp.zeros_like(table[6:8])
        table[8, 12:16] = jnp.zeros_like(table[8, 12:16])
        pnear[5:8] = jnp.zeros_like(pnear[5:8])
        dnear[5:8] = jnp.zeros_like(dnear[5:8])

    groups = lon // 16
    north_band, south_band = lax.rem(band + bands - 1, bands), lax.rem(band + 1, bands)
    cuts = ((0, 1), (groups - 1, 1), (1, groups - 2))
    g_north = [
        remote(
            table.at[pl.ds(0, 2), pl.ds(a, n)], table.at[pl.ds(6, 2), pl.ds(a, n)], G_NORTH + i, north_band, patch
        )
        for i, (a, n) in enumerate(cuts)
    ]
    g_south = [
        remote(
            table.at[pl.ds(2, 2), pl.ds(a, n)], table.at[pl.ds(4, 2), pl.ds(a, n)], G_SOUTH + i, south_band, patch
        )
        for i, (a, n) in enumerate(cuts)
    ]
    g_west = remote(table.at[pl.ds(0, 4), 0], table.at[8, pl.ds(4, 4)], G_WEST, band, west)
    g_east = remote(table.at[pl.ds(0, 4), groups - 1], table.at[8, pl.ds(0, 4)], G_EAST, band, east)
    g_north_on = [
        remote(table.at[pl.ds(4, 2), 0], table.at[8, pl.ds(10, 2)], G_FORWARD, band, west),
        remote(table.at[pl.ds(4, 2), groups - 1], table.at[8, pl.ds(8, 2)], G_FORWARD + 1, band, east),
    ]
    g_south_on = [
        remote(table.at[pl.ds(6, 2), 0], table.at[8, pl.ds(14, 2)], G_FORWARD + 2, band, west),
        remote(table.at[pl.ds(6, 2), groups - 1], table.at[8, pl.ds(12, 2)], G_FORWARD + 3, band, east),
    ]

    def near_copies(own, near, side, forward):
        rows = own.at[pl.ds(0, BORDER)]
        north = remote(rows, near.at[6], side, north_band, patch)
        south = remote(rows, near.at[1], side + 1, south_band, patch)
        flat = [remote(rows, near.at[4], side + 2, band, west), remote(rows, near.at[3], side + 3, band, east)]
        north_on = [
            remote(near.at[1], near.at[2], forward, band, west),
            remote(near.at[1], near.at[0], forward + 1, band, east),
        ]
        south_on = [
            remote(near.at[6], near.at[7], forward + 2, band, west),
            remote(near.at[6], near.at[5], forward + 3, band, east),
        ]
        return [north], [south], flat, north_on, south_on

    def when_all(condition, copies, method):
        @pl.when(condition)
        def _():
            for copy in copies:
                getattr(copy, method)()

    def start_sides(north, south, flat):
        when_all(has_north, north, "start")
        when_all(has_south, south, "start")
        for copy in flat:
            copy.start()

    def pass_on(from_south, from_north, north_on, south_on):
        when_all(has_north, from_north, "wait_recv")
        when_all(has_north, north_on, "start")
        when_all(has_south, from_south, "wait_recv")
        when_all(has_south, south_on, "start")

    def finish(north, south, flat, north_on, south_on):
        for copy in flat:
            copy.wait_recv()
        when_all(has_north, north_on, "wait_recv")
        when_all(has_south, south_on, "wait_recv")
        when_all(has_north, north, "wait_send")
        when_all(has_south, south, "wait_send")
        for copy in flat:
            copy.wait_send()
        when_all(has_north, north_on, "wait_send")
        when_all(has_south, south_on, "wait_send")

    def loop(count, step):
        def one(i, carry):
            step(i)
            return carry

        lax.fori_loop(0, count, one, 0)

    def at(i):
        return pl.ds(pl.multiple_of(i * ROWS, ROWS), ROWS)

    grid_steps = lat * lon // ROWS

    def grid_rows(i):
        return grid[pl.ds(i * half_lat, half_lat)].reshape(ROWS, latent)

    need("grid", "e0")

    def send_step(i):
        rows = dot(grid_rows(i), encw[0]).astype(BF)
        table[pl.ds(i * half_lat, half_lat)] = rows.reshape(half_lat, groups, 16, latent)

    loop(grid_steps, send_step)
    pl.semaphore_wait(barrier, bands - 1 + len(greeted))
    start_sides(g_north, g_south, [g_west, g_east])

    need("e78")

    def self_step(i):
        rows = grid_rows(i)
        hidden = silu(dot(rows, encw[7])).astype(BF)
        gnext[at(i)] = (rows.astype(F32) + layer_norm(dot(hidden, encw[8]))).astype(BF)

    loop(grid_steps, self_step)
    need("mesh", "e12")
    mrecv[...] = dot(mesh[...], encw[1]).astype(BF)
    pass_on(g_north[:2], g_south[:2], g_north_on, g_south_on)

    width = lon + 2 * HALO

    def grid_place(s):
        i = jnp.zeros_like(s)
        for k in range(1, lat + 2 * HALO):
            i = i + (s >= k * width).astype(jnp.int32)
        j = s - i * width
        north, south = i < HALO, i >= lat + HALO
        line = jnp.where(north, i + 4, jnp.where(south, i, i - 2))
        inner = line * lon + j - HALO
        left = jnp.where(north, i + 8, jnp.where(south, i + 6, i - 2)) * 16 + j + 14
        right = jnp.where(north, i + 10, jnp.where(south, i + 8, i + 2)) * 16 + j - (lon + HALO)
        edge = 8 * lon + jnp.where(j < HALO, left, right)
        return jnp.where((j < HALO) | (j >= lon + HALO), edge, inner)

    need("gs", "gr", "gf")

    def enc_own(i):
        place = columns_of(grid_place(gsend[:, at(i)]))
        recv = columns_of(grecv[:, at(i)])
        left = jnp.concatenate([gfeat[at(i)], pick(place, 0, 4 * lon), pick(recv, 0, nodes)], axis=1)
        right = jnp.concatenate([encw[2], table[0:4].reshape(4 * lon, latent), mrecv[...]], axis=0)
        pre_g[at(i)] = dot(left, right)

    loop(gfeat.shape[0] // ROWS, enc_own)
    need("p2", "pf")

    def proc_feat(i):
        pre_p[at(i)] = dot(pfeat[at(i)], procw[2])

    loop(pfeat.shape[0] // ROWS, proc_feat)
    need("d", "df", "ds")

    def dec_part(i):
        recv = dot(gnext[at(i)], decw[1]).astype(BF).astype(F32)
        for k in range(3):
            rows = dfeat[k, pl.ds(i * half_lat, half_lat)].reshape(ROWS, latent)
            pre_d[k, at(i)] = dot(rows, decw[2]) + recv

    loop(grid_steps, dec_part)

    when_all(has_south, g_north[2:], "wait_recv")
    when_all(has_north, g_south[2:], "wait_recv")
    finish(g_north, g_south, [g_west, g_east], g_north_on, g_south_on)
    need("e36")
    total[...] = jnp.zeros_like(total)
    live = blocks[band, patch] * 128

    def enc_edges(i):
        place = columns_of(grid_place(gsend[:, at(i)]))
        before = pre_g[at(i)] + dot(pick(place, 4 * lon, 5 * lon), table[4:9].reshape(5 * lon, latent))
        message = layer_norm(dot(silu(before).astype(BF), encw[3])).astype(BF)
        edge = lax.broadcasted_iota(jnp.int32, (1, ROWS), 1) + i * ROWS
        receiver = jnp.where(edge < live, grecv[:, at(i)], -1)
        total[...] += dot(scatter(receiver, nodes), message)

    loop(gfeat.shape[0] // ROWS, enc_edges)

    def mesh_step(current, weights, first):
        before = dot(current, weights[first]) + dot(total[...].astype(BF), weights[first + 1])
        hidden = silu(before).astype(BF)
        return (current.astype(F32) + layer_norm(dot(hidden, weights[first + 2]))).astype(BF)

    mnext[...] = mesh_step(mesh[...], encw, 4)

    need("p01")
    pown[...] = dot(mnext[...], procw[0]).astype(BF)
    pcoarse[patch, band] = pown[nodes - COARSE_DEV :]
    p_north, p_south, p_flat, p_north_on, p_south_on = near_copies(pown, pnear, P_SIDE, P_FORWARD)
    start_sides(p_north, p_south, p_flat)
    columns = []
    for k in range(1, bands):
        own = pcoarse.at[patch, band]
        there = pcoarse.at[patch, lax.rem(band + bands - k, bands)]
        columns.append(
            (
                remote(own, own, C_BASE + k, lax.rem(band + k, bands), patch),
                remote(there, there, C_BASE + k, lax.rem(band + k, bands), patch),
            )
        )
    for out_copy, _ in columns:
        out_copy.start()
    precv_rows[...] = dot(mnext[...], procw[1]).astype(BF)
    need("ps", "pr")

    shift = patches.bit_length() - 1

    def node_place(s):
        q = s >> 8
        slot = jnp.where(q > 4, q - 1, q)
        near = jnp.where(q == 4, s - 4 * nodes, nodes + slot * BORDER + (s & (nodes - 1)))
        c = s - 9 * nodes
        device = c >> 4
        distant = ((device & (patches - 1)) * bands + (device >> shift)) * COARSE_DEV + (c & (COARSE_DEV - 1))
        return jnp.where(c < 0, near, distant + nodes + 8 * BORDER)

    def proc_own(i):
        place = columns_of(node_place(psend[:, at(i)]))
        recv = columns_of(precv[:, at(i)])
        left = jnp.concatenate([pick(place, 0, nodes), pick(recv, 0, nodes)], axis=1)
        right = jnp.concatenate([pown[...], precv_rows[...]], axis=0)
        pre_p[at(i)] = pre_p[at(i)] + dot(left, right)

    pass_on(p_north, p_south, p_north_on, p_south_on)
    for _, in_copy in columns:
        in_copy.wait_recv()
    cores = 2
    count = patches // cores
    base = C_BASE + bands
    mate = patch + 1 - 2 * lax.rem(patch, 2)
    across, over = [], []
    for k in range(count):
        column = lax.rem(patch + patches - cores * k, patches)
        mate_column = lax.rem(mate + patches - cores * k, patches)
        src, got = pcoarse.at[column], pcoarse.at[mate_column]
        over.append(
            (remote(src, src, base + count + k, band, mate), remote(got, got, base + count + k, band, mate))
        )
        if k:
            to = lax.rem(patch + cores * k, patches)
            own = pcoarse.at[patch]
            across.append((remote(own, own, base + k, band, to), remote(src, src, base + k, band, to)))
    for out_copy, _ in across:
        out_copy.start()
    over[0][0].start()
    loop(pfeat.shape[0] // ROWS, proc_own)
    for k, (_, in_copy) in enumerate(across):
        in_copy.wait_recv()
        over[k + 1][0].start()

    def dec_update(i):
        upd[at(i)] = dot(gnext[at(i)], decw[4])

    loop(grid_steps, dec_update)
    for _, in_copy in over:
        in_copy.wait_recv()
    for out_copy, _ in columns + across + over:
        out_copy.wait_send()
    finish(p_north, p_south, p_flat, p_north_on, p_south_on)

    need("p36")
    total[...] = jnp.zeros_like(total)
    far = 8 * BORDER + bands * patches * COARSE_DEV

    def proc_edges(i):
        place = columns_of(node_place(psend[:, at(i)]))
        right = jnp.concatenate(
            [pnear[...].reshape(8 * BORDER, latent), pcoarse[...].reshape(far - 8 * BORDER, latent)], axis=0
        )
        before = pre_p[at(i)] + dot(pick(place, nodes, far), right)
        message = layer_norm(dot(silu(before).astype(BF), procw[3])).astype(BF)
        total[...] += dot(scatter(precv[:, at(i)], nodes), message)

    loop(pfeat.shape[0] // ROWS, proc_edges)
    last = mesh_step(mnext[...], procw, 4)

    down[...] = dot(last, decw[0]).astype(BF)
    d_north, d_south, d_flat, d_north_on, d_south_on = near_copies(down, dnear, D_SIDE, D_FORWARD)
    start_sides(d_north, d_south, d_flat)

    def dec_columns(k, i):
        rows = [dsend[k, pl.ds(i * half_lat + r, 1), :] for r in range(half_lat)]
        return columns_of(node_place(jnp.concatenate(rows, axis=1)))

    def dec_own(i):
        for k in range(3):
            pre_d[k, at(i)] = pre_d[k, at(i)] + dot(pick(dec_columns(k, i), 0, nodes), down[...])

    dec_own(0)
    pass_on(d_north, d_south, d_north_on, d_south_on)
    dec_own(1)
    finish(d_north, d_south, d_flat, d_north_on, d_south_on)

    def dec_edges(i):
        near = dnear[...].reshape(8 * BORDER, latent)
        summed = jnp.zeros((ROWS, latent), F32)
        for k in range(3):
            before = pre_d[k, at(i)] + dot(pick(dec_columns(k, i), nodes, 8 * BORDER), near)
            message = layer_norm(dot(silu(before).astype(BF), decw[3])).astype(BF)
            summed = summed + message.astype(F32)
        hidden = silu(upd[at(i)] + dot(summed.astype(BF), decw[5])).astype(BF)
        rows = (gnext[at(i)].astype(F32) + layer_norm(dot(hidden, decw[6]))).astype(BF)
        result[pl.ds(i * half_lat, half_lat)] = rows.reshape(half_lat, lon, latent)

    stores = []
    for i in range(grid_steps):
        dec_edges(i)
        part = pl.ds(i * half_lat, half_lat)
        stores.append(pltpu.make_async_copy(result.at[part], out.at[part], out_sem.at[i]))
        stores[-1].start()
    for copy in stores:
        copy.wait()


def solution(mesh):
    bands, patches = mesh.shape["band"], mesh.shape["patch"]

    def shards(grid, mesh_state, gfeat, gsend, grecv, blocks, pfeat, psend, precv, dfeat, dsend, encw, procw, decw):
        lat, lon, latent = grid.shape
        nodes = mesh_state.shape[2]
        edges, pedges = gfeat.shape[2], pfeat.shape[2]
        cells = lat * lon
        any_spec = pl.BlockSpec(memory_space=pl.ANY)
        vmem = pltpu.VMEM
        copies = C_BASE + bands + patches
        return pl.pallas_call(
            functools.partial(body, bands, patches),
            out_shape=jax.ShapeDtypeStruct(grid.shape, BF),
            in_specs=[any_spec] * 5 + [pl.BlockSpec(memory_space=pltpu.SMEM)] + [any_spec] * 8,
            out_specs=any_spec,
            scratch_shapes=[
                vmem(grid.shape, BF),
                vmem((nodes, latent), BF),
                vmem((edges, latent), BF),
                vmem((1, edges), jnp.int32),
                vmem((1, edges), jnp.int32),
                vmem((pedges, latent), BF),
                vmem((1, pedges), jnp.int32),
                vmem((1, pedges), jnp.int32),
                vmem(dfeat.shape, BF),
                vmem(dsend.shape, jnp.int32),
                vmem(encw.shape, BF),
                vmem(procw.shape, BF),
                vmem(decw.shape, BF),
                vmem((9, lon // 16, 16, latent), BF),
                vmem((nodes, latent), BF),
                vmem((cells, latent), BF),
                vmem((edges, latent), F32),
                vmem((pedges, latent), F32),
                vmem((3, cells, latent), F32),
                vmem((cells, latent), F32),
                vmem((nodes, latent), F32),
                vmem((nodes, latent), BF),
                vmem((nodes, latent), BF),
                vmem((8, BORDER, latent), BF),
                vmem((patches, bands, COARSE_DEV, latent), BF),
                vmem((nodes, latent), BF),
                vmem((nodes, latent), BF),
                vmem((8, BORDER, latent), BF),
                vmem(grid.shape, BF),
                pltpu.SemaphoreType.DMA((18,)),
                pltpu.SemaphoreType.DMA((2,)),
                pltpu.SemaphoreType.DMA((copies,)),
                pltpu.SemaphoreType.DMA((copies,)),
            ],
            compiler_params=pltpu.CompilerParams(
                collective_id=0, has_side_effects=True, vmem_limit_bytes=62 * 1024 * 1024
            ),
            cost_estimate=pl.CostEstimate(flops=24 * 10**9, bytes_accessed=24 * 10**6, transcendentals=5 * 10**6),
        )(grid, mesh_state, gfeat, gsend, grecv, blocks, pfeat, psend, precv, dfeat, dsend, encw, procw, decw)

    placed = (
        P("band", "patch", None),
        P("band", "patch", None, None),
        P("band", "patch", None, None),
        P("band", "patch", None),
        P("band", "patch", None),
        P(),
        P("band", "patch", None, None),
        P("band", "patch", None),
        P("band", "patch", None),
        P(None, "band", "patch", None),
        P(None, "band", "patch"),
        P(),
        P(),
        P(),
    )
    return jax.shard_map(
        shards, mesh=mesh, in_specs=placed, out_specs=P("band", "patch", None), check_vma=False
    )
```

time: 432 us -> 78.1 us (0.18)
  the two profiles are of different devices: /device:TPU:0 before, /device:TPU:9 now
where the time goes in v1:
time: 78.1 us; the launch traced here: 77 us
  Pallas kernels  73.4 us (94%)
  local copies, waits for them, and re-layouts  3.61 us (5%)
    pallas_call x1, Pallas kernels, shards(): pl.pallas_call(functools.partial(body, bands, patches), out_shape=jax.Sha...  73.4 us
    unnamed x2, local copies, waits for them, and re-layouts  3.61 us

profile of v1, /device:TPU:9, one launch (start us, length us, event | category | flops | bytes accessed | tf_op | source)
XLA Modules:
  0.0 77.0 jit_solution(2298717124887180483)
XLA Ops:
  0.0 1.3 %copy.15.blocks = s32[8,4]{1,0:T(8,128)} copy(s32[8,4]{0,1:T(4,128)} %param.19) | data formatting | bytes 256 | tf_op args[5]
  1.3 73.4 %shard_map.136 = bf16[4,256,512]{2,1,0:T(8,128)(2,1)} custom-call(bf16[4,256,512]{2,1,0:T(8,128)(2,1)} %grid_in.1, bf16[1,1,256,512]{3,2,1,0:T(8,128)(2,1)} %mesh_in.1, bf16[1,1,2048,512]{3,2,1,0:T(8,128)(2,1)} %gfeat_in.1, s32[1,1,2048]{2,1,0:T(1,128)} %gsend_in.1, s32[1,1,2048]{2,1,0:T(1,128)} %grecv_in.1, s32[8,4]{1,0:T(8,128)} %copy.15.blocks, ...), custom_call_target="tpu_custom_call" | custom-call | flops 24000000000 | bytes 24000000 | tf_op jit(solution)/shard_map/pallas_call | solution.py:497
  74.7 2.3 %copy.17 = bf16[4,256,512]{2,1,0:T(8,128)(2,1)} copy(bf16[4,256,512]{2,1,0:T(8,128)(2,1)} %shard_map.136) | data formatting | bytes 2097152

commit v2 on v1

--- a/solution.py
+++ b/solution.py
@@ -18,8 +18,8 @@
 
 G_NORTH, G_SOUTH, G_WEST, G_EAST = 0, 3, 6, 7
 G_FORWARD = 8
-P_SIDE, P_FORWARD, D_SIDE, D_FORWARD = 12, 16, 20, 24
-C_BASE = 28
+P_FIRST, D_FIRST = 12, 26
+C_BASE = 40
 
 
 def dot(a, b):
@@ -65,7 +65,7 @@
     gfeat_in,
     gsend_in,
     grecv_in,
-    blocks,
+    blocks_in,
     pfeat_in,
     psend_in,
     precv_in,
@@ -91,16 +91,21 @@
     table,
     mrecv,
     gnext,
-    pre_g,
-    pre_p,
+    pre_e,
     pre_d,
     upd,
+    base,
+    cols_g,
+    cols_p,
+    cols_d,
+    blocks,
     total,
     mnext,
     pown,
     pnear,
     pcoarse,
     precv_rows,
+    recv_d,
     down,
     dnear,
     result,
@@ -123,23 +128,24 @@
         copy.start()
         loads[name] = copy
 
+    load("e0", encw_in.at[0], encw.at[0])
     load("grid", grid_in, grid)
-    load("e0", encw_in.at[0], encw.at[0])
     load("e78", encw_in.at[pl.ds(7, 2)], encw.at[pl.ds(7, 2)])
     load("mesh", mesh_in.at[0, 0], mesh)
     load("e12", encw_in.at[pl.ds(1, 2)], encw.at[pl.ds(1, 2)])
     load("gs", gsend_in.at[0], gsend)
     load("gr", grecv_in.at[0], grecv)
+    load("ps", psend_in.at[0], psend)
+    load("pr", precv_in.at[0], precv)
+    load("ds", dsend_in, dsend)
+    load("blocks", blocks_in, blocks)
     load("gf", gfeat_in.at[0, 0], gfeat)
     load("p2", procw_in.at[2], procw.at[2])
     load("pf", pfeat_in.at[0, 0], pfeat)
     load("e36", encw_in.at[pl.ds(3, 4)], encw.at[pl.ds(3, 4)])
     load("p01", procw_in.at[pl.ds(0, 2)], procw.at[pl.ds(0, 2)])
-    load("ps", psend_in.at[0], psend)
-    load("pr", precv_in.at[0], precv)
     load("d", decw_in, decw)
     load("df", dfeat_in, dfeat)
-    load("ds", dsend_in, dsend)
     load("p36", procw_in.at[pl.ds(3, 4)], procw.at[pl.ds(3, 4)])
 
     def need(*names):
@@ -207,20 +213,30 @@
         remote(table.at[pl.ds(6, 2), groups - 1], table.at[8, pl.ds(12, 2)], G_FORWARD + 3, band, east),
     ]
 
-    def near_copies(own, near, side, forward):
+    chunk = BORDER // 2
+
+    def near_copies(own, near, first):
         rows = own.at[pl.ds(0, BORDER)]
-        north = remote(rows, near.at[6], side, north_band, patch)
-        south = remote(rows, near.at[1], side + 1, south_band, patch)
-        flat = [remote(rows, near.at[4], side + 2, band, west), remote(rows, near.at[3], side + 3, band, east)]
-        north_on = [
-            remote(near.at[1], near.at[2], forward, band, west),
-            remote(near.at[1], near.at[0], forward + 1, band, east),
-        ]
-        south_on = [
-            remote(near.at[6], near.at[7], forward + 2, band, west),
-            remote(near.at[6], near.at[5], forward + 3, band, east),
-        ]
-        return [north], [south], flat, north_on, south_on
+        flat = [remote(rows, near.at[4], first, band, west), remote(rows, near.at[3], first + 1, band, east)]
+        norths, souths, norths_on, souths_on = [], [], [], []
+        for c in range(2):
+            n = first + 2 + 6 * c
+            part = pl.ds(c * chunk, chunk)
+            norths.append(remote(own.at[part], near.at[6, part], n, north_band, patch))
+            souths.append(remote(own.at[part], near.at[1, part], n + 1, south_band, patch))
+            norths_on += [
+                remote(near.at[1, part], near.at[2, part], n + 2, band, west),
+                remote(near.at[1, part], near.at[0, part], n + 3, band, east),
+            ]
+            souths_on += [
+                remote(near.at[6, part], near.at[7, part], n + 4, band, west),
+                remote(near.at[6, part], near.at[5, part], n + 5, band, east),
+            ]
+        return norths, souths, flat, norths_on, souths_on
+
+    def pass_chunk(c, norths, souths, flat, norths_on, souths_on):
+        two = slice(2 * c, 2 * c + 2)
+        pass_on(norths[c : c + 1], souths[c : c + 1], norths_on[two], souths_on[two])
 
     def when_all(condition, copies, method):
         @pl.when(condition)
@@ -252,12 +268,12 @@
         when_all(has_north, north_on, "wait_send")
         when_all(has_south, south_on, "wait_send")
 
-    def loop(count, step):
+    def loop(count, step, unroll=1):
         def one(i, carry):
             step(i)
             return carry
 
-        lax.fori_loop(0, count, one, 0)
+        lax.fori_loop(0, count, one, 0, unroll=unroll)
 
     def at(i):
         return pl.ds(pl.multiple_of(i * ROWS, ROWS), ROWS)
@@ -273,9 +289,14 @@
         rows = dot(grid_rows(i), encw[0]).astype(BF)
         table[pl.ds(i * half_lat, half_lat)] = rows.reshape(half_lat, groups, 16, latent)
 
-    loop(grid_steps, send_step)
+    send_step(0)
     pl.semaphore_wait(barrier, bands - 1 + len(greeted))
-    start_sides(g_north, g_south, [g_west, g_east])
+    when_all(has_north, g_north, "start")
+    for i in range(1, grid_steps):
+        send_step(i)
+    when_all(has_south, g_south, "start")
+    g_west.start()
+    g_east.start()
 
     need("e78")
 
@@ -287,6 +308,8 @@
     loop(grid_steps, self_step)
     need("mesh", "e12")
     mrecv[...] = dot(mesh[...], encw[1]).astype(BF)
+    need("e36")
+    base[...] = dot(mesh[...], encw[4])
     pass_on(g_north[:2], g_south[:2], g_north_on, g_south_on)
 
     width = lon + 2 * HALO
@@ -304,61 +327,77 @@
         edge = 8 * lon + jnp.where(j < HALO, left, right)
         return jnp.where((j < HALO) | (j >= lon + HALO), edge, inner)
 
+    shift = patches.bit_length() - 1
+
+    def node_place(s):
+        q = s >> 8
+        slot = jnp.where(q > 4, q - 1, q)
+        near = jnp.where(q == 4, s - 4 * nodes, nodes + slot * BORDER + (s & (nodes - 1)))
+        c = s - 9 * nodes
+        device = c >> 4
+        distant = ((device & (patches - 1)) * bands + (device >> shift)) * COARSE_DEV + (c & (COARSE_DEV - 1))
+        return jnp.where(c < 0, near, distant + nodes + 8 * BORDER)
+
+    def dec_columns(k, i):
+        rows = [dsend[k, pl.ds(i * half_lat + r, 1), :] for r in range(half_lat)]
+        return columns_of(node_place(jnp.concatenate(rows, axis=1)))
+
     need("gs", "gr", "gf")
 
     def enc_own(i):
         place = columns_of(grid_place(gsend[:, at(i)]))
+        cols_g[at(i)] = place
         recv = columns_of(grecv[:, at(i)])
         left = jnp.concatenate([gfeat[at(i)], pick(place, 0, 4 * lon), pick(recv, 0, nodes)], axis=1)
         right = jnp.concatenate([encw[2], table[0:4].reshape(4 * lon, latent), mrecv[...]], axis=0)
-        pre_g[at(i)] = dot(left, right)
+        pre_e[at(i)] = dot(left, right)
 
     loop(gfeat.shape[0] // ROWS, enc_own)
-    need("p2", "pf")
-
-    def proc_feat(i):
-        pre_p[at(i)] = dot(pfeat[at(i)], procw[2])
-
-    loop(pfeat.shape[0] // ROWS, proc_feat)
-    need("d", "df", "ds")
-
-    def dec_part(i):
-        recv = dot(gnext[at(i)], decw[1]).astype(BF).astype(F32)
+    need("ps", "pr", "ds")
+
+    def proc_place(i):
+        cols_p[at(i)] = columns_of(node_place(psend[:, at(i)]))
+
+    loop(pfeat.shape[0] // ROWS, proc_place)
+
+    def dec_place(i):
         for k in range(3):
-            rows = dfeat[k, pl.ds(i * half_lat, half_lat)].reshape(ROWS, latent)
-            pre_d[k, at(i)] = dot(rows, decw[2]) + recv
-
-    loop(grid_steps, dec_part)
+            cols_d[k, at(i)] = dec_columns(k, i)
+
+    loop(grid_steps, dec_place)
+    need("d")
+
+    def dec_grid(i):
+        recv_d[at(i)] = dot(gnext[at(i)], decw[1]).astype(BF)
+
+    loop(grid_steps, dec_grid)
+    need("blocks", "p2", "pf", "p01", "df")
 
     when_all(has_south, g_north[2:], "wait_recv")
     when_all(has_north, g_south[2:], "wait_recv")
     finish(g_north, g_south, [g_west, g_east], g_north_on, g_south_on)
-    need("e36")
     total[...] = jnp.zeros_like(total)
     live = blocks[band, patch] * 128
 
     def enc_edges(i):
-        place = columns_of(grid_place(gsend[:, at(i)]))
-        before = pre_g[at(i)] + dot(pick(place, 4 * lon, 5 * lon), table[4:9].reshape(5 * lon, latent))
+        before = pre_e[at(i)] + dot(pick(cols_g[at(i)], 4 * lon, 5 * lon), table[4:9].reshape(5 * lon, latent))
         message = layer_norm(dot(silu(before).astype(BF), encw[3])).astype(BF)
         edge = lax.broadcasted_iota(jnp.int32, (1, ROWS), 1) + i * ROWS
         receiver = jnp.where(edge < live, grecv[:, at(i)], -1)
         total[...] += dot(scatter(receiver, nodes), message)
 
-    loop(gfeat.shape[0] // ROWS, enc_edges)
+    loop(gfeat.shape[0] // ROWS, enc_edges, 2)
 
     def mesh_step(current, weights, first):
-        before = dot(current, weights[first]) + dot(total[...].astype(BF), weights[first + 1])
+        before = base[...] + dot(total[...].astype(BF), weights[first + 1])
         hidden = silu(before).astype(BF)
         return (current.astype(F32) + layer_norm(dot(hidden, weights[first + 2]))).astype(BF)
 
     mnext[...] = mesh_step(mesh[...], encw, 4)
 
-    need("p01")
     pown[...] = dot(mnext[...], procw[0]).astype(BF)
     pcoarse[patch, band] = pown[nodes - COARSE_DEV :]
-    p_north, p_south, p_flat, p_north_on, p_south_on = near_copies(pown, pnear, P_SIDE, P_FORWARD)
-    start_sides(p_north, p_south, p_flat)
+    p_near = near_copies(pown, pnear, P_FIRST)
     columns = []
     for k in range(1, bands):
         own = pcoarse.at[patch, band]
@@ -371,33 +410,27 @@
         )
     for out_copy, _ in columns:
         out_copy.start()
+    start_sides(*p_near[:3])
     precv_rows[...] = dot(mnext[...], procw[1]).astype(BF)
-    need("ps", "pr")
-
-    shift = patches.bit_length() - 1
-
-    def node_place(s):
-        q = s >> 8
-        slot = jnp.where(q > 4, q - 1, q)
-        near = jnp.where(q == 4, s - 4 * nodes, nodes + slot * BORDER + (s & (nodes - 1)))
-        c = s - 9 * nodes
-        device = c >> 4
-        distant = ((device & (patches - 1)) * bands + (device >> shift)) * COARSE_DEV + (c & (COARSE_DEV - 1))
-        return jnp.where(c < 0, near, distant + nodes + 8 * BORDER)
+    need("p36")
+    base[...] = dot(mnext[...], procw[4])
 
     def proc_own(i):
-        place = columns_of(node_place(psend[:, at(i)]))
         recv = columns_of(precv[:, at(i)])
-        left = jnp.concatenate([pick(place, 0, nodes), pick(recv, 0, nodes)], axis=1)
-        right = jnp.concatenate([pown[...], precv_rows[...]], axis=0)
-        pre_p[at(i)] = pre_p[at(i)] + dot(left, right)
-
-    pass_on(p_north, p_south, p_north_on, p_south_on)
+        left = jnp.concatenate([pfeat[at(i)], pick(cols_p[at(i)], 0, nodes), pick(recv, 0, nodes)], axis=1)
+        right = jnp.concatenate([procw[2], pown[...], precv_rows[...]], axis=0)
+        pre_e[at(i)] = dot(left, right)
+
+    def dec_update(i):
+        upd[at(i)] = dot(gnext[at(i)], decw[4])
+
+    loop(grid_steps, dec_update)
+
     for _, in_copy in columns:
         in_copy.wait_recv()
     cores = 2
     count = patches // cores
-    base = C_BASE + bands
+    first_id = C_BASE + bands
     mate = patch + 1 - 2 * lax.rem(patch, 2)
     across, over = [], []
     for k in range(count):
@@ -405,68 +438,68 @@
         mate_column = lax.rem(mate + patches - cores * k, patches)
         src, got = pcoarse.at[column], pcoarse.at[mate_column]
         over.append(
-            (remote(src, src, base + count + k, band, mate), remote(got, got, base + count + k, band, mate))
+            (remote(src, src, first_id + count + k, band, mate), remote(got, got, first_id + count + k, band, mate))
         )
         if k:
             to = lax.rem(patch + cores * k, patches)
             own = pcoarse.at[patch]
-            across.append((remote(own, own, base + k, band, to), remote(src, src, base + k, band, to)))
+            across.append((remote(own, own, first_id + k, band, to), remote(src, src, first_id + k, band, to)))
     for out_copy, _ in across:
         out_copy.start()
     over[0][0].start()
-    loop(pfeat.shape[0] // ROWS, proc_own)
+    pass_chunk(0, *p_near)
+    half = pfeat.shape[0] // ROWS // 2
+    loop(half, proc_own)
+    pass_chunk(1, *p_near)
     for k, (_, in_copy) in enumerate(across):
         in_copy.wait_recv()
         over[k + 1][0].start()
 
-    def dec_update(i):
-        upd[at(i)] = dot(gnext[at(i)], decw[4])
-
-    loop(grid_steps, dec_update)
+    loop(pfeat.shape[0] // ROWS - half, lambda i: proc_own(i + half))
     for _, in_copy in over:
         in_copy.wait_recv()
     for out_copy, _ in columns + across + over:
         out_copy.wait_send()
-    finish(p_north, p_south, p_flat, p_north_on, p_south_on)
-
-    need("p36")
+    finish(*p_near)
+
     total[...] = jnp.zeros_like(total)
     far = 8 * BORDER + bands * patches * COARSE_DEV
 
     def proc_edges(i):
-        place = columns_of(node_place(psend[:, at(i)]))
         right = jnp.concatenate(
             [pnear[...].reshape(8 * BORDER, latent), pcoarse[...].reshape(far - 8 * BORDER, latent)], axis=0
         )
-        before = pre_p[at(i)] + dot(pick(place, nodes, far), right)
+        before = pre_e[at(i)] + dot(pick(cols_p[at(i)], nodes, far), right)
         message = layer_norm(dot(silu(before).astype(BF), procw[3])).astype(BF)
         total[...] += dot(scatter(precv[:, at(i)], nodes), message)
 
-    loop(pfeat.shape[0] // ROWS, proc_edges)
+    loop(pfeat.shape[0] // ROWS, proc_edges, 2)
     last = mesh_step(mnext[...], procw, 4)
 
     down[...] = dot(last, decw[0]).astype(BF)
-    d_north, d_south, d_flat, d_north_on, d_south_on = near_copies(down, dnear, D_SIDE, D_FORWARD)
-    start_sides(d_north, d_south, d_flat)
-
-    def dec_columns(k, i):
-        rows = [dsend[k, pl.ds(i * half_lat + r, 1), :] for r in range(half_lat)]
-        return columns_of(node_place(jnp.concatenate(rows, axis=1)))
+    d_near = near_copies(down, dnear, D_FIRST)
+    start_sides(*d_near[:3])
 
     def dec_own(i):
+        recv = recv_d[at(i)].astype(F32)
+        right = jnp.concatenate([decw[2], down[...]], axis=0)
         for k in range(3):
-            pre_d[k, at(i)] = pre_d[k, at(i)] + dot(pick(dec_columns(k, i), 0, nodes), down[...])
+            rows = dfeat[k, pl.ds(i * half_lat, half_lat)].reshape(ROWS, latent)
+            left = jnp.concatenate([rows, pick(cols_d[k, at(i)], 0, nodes)], axis=1)
+            pre_d[k, at(i)] = dot(left, right) + recv
 
     dec_own(0)
-    pass_on(d_north, d_south, d_north_on, d_south_on)
-    dec_own(1)
-    finish(d_north, d_south, d_flat, d_north_on, d_south_on)
+    pass_chunk(0, *d_near)
+    for i in range(1, grid_steps):
+        dec_own(i)
+    pass_chunk(1, *d_near)
+    finish(*d_near)
 
     def dec_edges(i):
         near = dnear[...].reshape(8 * BORDER, latent)
         summed = jnp.zeros((ROWS, latent), F32)
         for k in range(3):
-            before = pre_d[k, at(i)] + dot(pick(dec_columns(k, i), nodes, 8 * BORDER), near)
+            before = pre_d[k, at(i)] + dot(pick(cols_d[k, at(i)], nodes, 8 * BORDER), near)
             message = layer_norm(dot(silu(before).astype(BF), decw[3])).astype(BF)
             summed = summed + message.astype(F32)
         hidden = silu(upd[at(i)] + dot(summed.astype(BF), decw[5])).astype(BF)
@@ -497,7 +530,7 @@
         return pl.pallas_call(
             functools.partial(body, bands, patches),
             out_shape=jax.ShapeDtypeStruct(grid.shape, BF),
-            in_specs=[any_spec] * 5 + [pl.BlockSpec(memory_space=pltpu.SMEM)] + [any_spec] * 8,
+            in_specs=[any_spec] * 14,
             out_specs=any_spec,
             scratch_shapes=[
                 vmem(grid.shape, BF),
@@ -516,20 +549,25 @@
                 vmem((9, lon // 16, 16, latent), BF),
                 vmem((nodes, latent), BF),
                 vmem((cells, latent), BF),
-                vmem((edges, latent), F32),
-                vmem((pedges, latent), F32),
+                vmem((max(edges, pedges), latent), F32),
                 vmem((3, cells, latent), F32),
                 vmem((cells, latent), F32),
+                vmem((nodes, latent), F32),
+                vmem((edges, 128), jnp.int16),
+                vmem((pedges, 128), jnp.int16),
+                vmem((3, cells, 128), jnp.int16),
+                pltpu.SMEM((bands, patches), jnp.int32),
                 vmem((nodes, latent), F32),
                 vmem((nodes, latent), BF),
                 vmem((nodes, latent), BF),
                 vmem((8, BORDER, latent), BF),
                 vmem((patches, bands, COARSE_DEV, latent), BF),
                 vmem((nodes, latent), BF),
+                vmem((cells, latent), BF),
                 vmem((nodes, latent), BF),
                 vmem((8, BORDER, latent), BF),
                 vmem(grid.shape, BF),
-                pltpu.SemaphoreType.DMA((18,)),
+                pltpu.SemaphoreType.DMA((19,)),
                 pltpu.SemaphoreType.DMA((2,)),
                 pltpu.SemaphoreType.DMA((copies,)),
                 pltpu.SemaphoreType.DMA((copies,)),

time: 78.1 us -> 74.1 us (0.949); the launches traced: 77 us -> 73.9 us
  Pallas kernels: 73.4 us -> 70.2 us
    pallas_call x1, Pallas kernels: 73.4 us -> 70.2 us  [shards(): pl.pallas_call(functools.partial(body, bands, patches), out_shape=jax.Sha...]
where the time goes in v2:
time: 74.1 us; the launch traced here: 73.9 us
  Pallas kernels  70.2 us (95%)
  local copies, waits for them, and re-layouts  3.61 us (5%)
    pallas_call x1, Pallas kernels, shards(): pl.pallas_call(functools.partial(body, bands, patches), out_shape=jax.Sha...  70.2 us
    unnamed x2, local copies, waits for them, and re-layouts  3.61 us

profile of v2, /device:TPU:9, one launch (start us, length us, event | category | flops | bytes accessed | tf_op | source)
XLA Modules:
  0.0 73.9 jit_solution(5306283791085083100)
XLA Ops:
  0.0 1.3 %copy.15.blocks_in = s32[8,4]{1,0:T(8,128)} copy(s32[8,4]{0,1:T(4,128)} %param.19) | data formatting | bytes 256 | tf_op args[5]
  1.3 70.2 %shard_map.136 = bf16[4,256,512]{2,1,0:T(8,128)(2,1)} custom-call(bf16[4,256,512]{2,1,0:T(8,128)(2,1)} %grid_in.1, bf16[1,1,256,512]{3,2,1,0:T(8,128)(2,1)} %mesh_in.1, bf16[1,1,2048,512]{3,2,1,0:T(8,128)(2,1)} %gfeat_in.1, s32[1,1,2048]{2,1,0:T(1,128)} %gsend_in.1, s32[1,1,2048]{2,1,0:T(1,128)} %grecv_in.1, s32[8,4]{1,0:T(8,128)} %copy.15.blocks_in, ...), custom_call_target="tpu_custom_call" | custom-call | flops 24000000000 | bytes 24000000 | tf_op jit(solution)/shard_map/pallas_call | solution.py:530
  71.6 2.3 %copy.17 = bf16[4,256,512]{2,1,0:T(8,128)(2,1)} copy(bf16[4,256,512]{2,1,0:T(8,128)(2,1)} %shard_map.136) | data formatting | bytes 2097152

commit v3 on v2

--- a/solution.py
+++ b/solution.py
@@ -16,10 +16,10 @@
 F32 = jnp.float32
 ROWS = 512
 
-G_NORTH, G_SOUTH, G_WEST, G_EAST = 0, 3, 6, 7
-G_FORWARD = 8
-P_FIRST, D_FIRST = 12, 26
-C_BASE = 40
+G_NORTH, G_SOUTH, G_WEST, G_EAST = 0, 4, 8, 9
+G_FORWARD = 10
+P_FIRST, D_FIRST = 14, 28
+C_BASE = 42
 
 
 def dot(a, b):
@@ -177,31 +177,38 @@
     def _():
         table[4:6] = jnp.zeros_like(table[4:6])
         table[8, 8:12] = jnp.zeros_like(table[8, 8:12])
-        pnear[0:3] = jnp.zeros_like(pnear[0:3])
-        dnear[0:3] = jnp.zeros_like(dnear[0:3])
+        pnear[0] = jnp.zeros_like(pnear[0])
+        pnear[4:6] = jnp.zeros_like(pnear[4:6])
+        dnear[0] = jnp.zeros_like(dnear[0])
+        dnear[4:6] = jnp.zeros_like(dnear[4:6])
 
     @pl.when(jnp.logical_not(has_south))
     def _():
         table[6:8] = jnp.zeros_like(table[6:8])
         table[8, 12:16] = jnp.zeros_like(table[8, 12:16])
-        pnear[5:8] = jnp.zeros_like(pnear[5:8])
-        dnear[5:8] = jnp.zeros_like(dnear[5:8])
+        pnear[1] = jnp.zeros_like(pnear[1])
+        pnear[6:8] = jnp.zeros_like(pnear[6:8])
+        dnear[1] = jnp.zeros_like(dnear[1])
+        dnear[6:8] = jnp.zeros_like(dnear[6:8])
 
     groups = lon // 16
     north_band, south_band = lax.rem(band + bands - 1, bands), lax.rem(band + 1, bands)
-    cuts = ((0, 1), (groups - 1, 1), (1, groups - 2))
-    g_north = [
-        remote(
-            table.at[pl.ds(0, 2), pl.ds(a, n)], table.at[pl.ds(6, 2), pl.ds(a, n)], G_NORTH + i, north_band, patch
-        )
-        for i, (a, n) in enumerate(cuts)
-    ]
-    g_south = [
-        remote(
-            table.at[pl.ds(2, 2), pl.ds(a, n)], table.at[pl.ds(4, 2), pl.ds(a, n)], G_SOUTH + i, south_band, patch
-        )
-        for i, (a, n) in enumerate(cuts)
-    ]
+    cuts = ((0, 2, 0, 1), (0, 2, groups - 1, 1), (0, 1, 1, groups - 2), (1, 1, 1, groups - 2))
+
+    def halo(start, landing, first, to_band):
+        return [
+            remote(
+                table.at[pl.ds(start + r, rows), pl.ds(g, n)],
+                table.at[pl.ds(landing + r, rows), pl.ds(g, n)],
+                first + i,
+                to_band,
+                patch,
+            )
+            for i, (r, rows, g, n) in enumerate(cuts)
+        ]
+
+    g_north = halo(0, 6, G_NORTH, north_band)
+    g_south = halo(2, 4, G_SOUTH, south_band)
     g_west = remote(table.at[pl.ds(0, 4), 0], table.at[8, pl.ds(4, 4)], G_WEST, band, west)
     g_east = remote(table.at[pl.ds(0, 4), groups - 1], table.at[8, pl.ds(0, 4)], G_EAST, band, east)
     g_north_on = [
@@ -217,20 +224,20 @@
 
     def near_copies(own, near, first):
         rows = own.at[pl.ds(0, BORDER)]
-        flat = [remote(rows, near.at[4], first, band, west), remote(rows, near.at[3], first + 1, band, east)]
+        flat = [remote(rows, near.at[3], first, band, west), remote(rows, near.at[2], first + 1, band, east)]
         norths, souths, norths_on, souths_on = [], [], [], []
         for c in range(2):
             n = first + 2 + 6 * c
             part = pl.ds(c * chunk, chunk)
-            norths.append(remote(own.at[part], near.at[6, part], n, north_band, patch))
-            souths.append(remote(own.at[part], near.at[1, part], n + 1, south_band, patch))
+            norths.append(remote(own.at[part], near.at[1, part], n, north_band, patch))
+            souths.append(remote(own.at[part], near.at[0, part], n + 1, south_band, patch))
             norths_on += [
-                remote(near.at[1, part], near.at[2, part], n + 2, band, west),
-                remote(near.at[1, part], near.at[0, part], n + 3, band, east),
+                remote(near.at[0, part], near.at[5, part], n + 2, band, west),
+                remote(near.at[0, part], near.at[4, part], n + 3, band, east),
             ]
             souths_on += [
-                remote(near.at[6, part], near.at[7, part], n + 4, band, west),
-                remote(near.at[6, part], near.at[5, part], n + 5, band, east),
+                remote(near.at[1, part], near.at[7, part], n + 4, band, west),
+                remote(near.at[1, part], near.at[6, part], n + 5, band, east),
             ]
         return norths, souths, flat, norths_on, souths_on
 
@@ -256,11 +263,13 @@
         when_all(has_south, from_south, "wait_recv")
         when_all(has_south, south_on, "start")
 
-    def finish(north, south, flat, north_on, south_on):
+    def arrived(flat, north_on, south_on):
         for copy in flat:
             copy.wait_recv()
         when_all(has_north, north_on, "wait_recv")
         when_all(has_south, south_on, "wait_recv")
+
+    def sent(north, south, flat, north_on, south_on):
         when_all(has_north, north, "wait_send")
         when_all(has_south, south, "wait_send")
         for copy in flat:
@@ -329,18 +338,24 @@
 
     shift = patches.bit_length() - 1
 
-    def node_place(s):
+    def node_place(s, coarse):
         q = s >> 8
-        slot = jnp.where(q > 4, q - 1, q)
-        near = jnp.where(q == 4, s - 4 * nodes, nodes + slot * BORDER + (s & (nodes - 1)))
+        slot = jnp.zeros_like(q)
+        for name, number in ((0, 4), (2, 5), (3, 2), (5, 3), (6, 6), (7, 1), (8, 7)):
+            slot = jnp.where(q == name, number, slot)
+        distant_rows = bands * patches * COARSE_DEV
+        shifted = jnp.where(slot >= 4, distant_rows, 0) + slot * BORDER if coarse else slot * BORDER
+        near = jnp.where(q == 4, s - 4 * nodes, nodes + shifted + (s & (nodes - 1)))
+        if not coarse:
+            return near
         c = s - 9 * nodes
         device = c >> 4
         distant = ((device & (patches - 1)) * bands + (device >> shift)) * COARSE_DEV + (c & (COARSE_DEV - 1))
-        return jnp.where(c < 0, near, distant + nodes + 8 * BORDER)
+        return jnp.where(c < 0, near, distant + nodes + 4 * BORDER)
 
     def dec_columns(k, i):
         rows = [dsend[k, pl.ds(i * half_lat + r, 1), :] for r in range(half_lat)]
-        return columns_of(node_place(jnp.concatenate(rows, axis=1)))
+        return columns_of(node_place(jnp.concatenate(rows, axis=1), False))
 
     need("gs", "gr", "gf")
 
@@ -356,7 +371,7 @@
     need("ps", "pr", "ds")
 
     def proc_place(i):
-        cols_p[at(i)] = columns_of(node_place(psend[:, at(i)]))
+        cols_p[at(i)] = columns_of(node_place(psend[:, at(i)], True))
 
     loop(pfeat.shape[0] // ROWS, proc_place)
 
@@ -373,14 +388,27 @@
     loop(grid_steps, dec_grid)
     need("blocks", "p2", "pf", "p01", "df")
 
-    when_all(has_south, g_north[2:], "wait_recv")
-    when_all(has_north, g_south[2:], "wait_recv")
-    finish(g_north, g_south, [g_west, g_east], g_north_on, g_south_on)
+    arrived([g_west, g_east], g_north_on, g_south_on)
+    when_all(has_south, g_north[2:3], "wait_recv")
+    when_all(has_north, g_south[2:3], "wait_recv")
+
+    def enc_first(i):
+        place = cols_g[at(i)]
+        left = jnp.concatenate([pick(place, n * lon, lon) for n in (4, 6, 8)], axis=1)
+        right = jnp.concatenate([table[n].reshape(lon, latent) for n in (4, 6, 8)], axis=0)
+        pre_e[at(i)] = pre_e[at(i)] + dot(left, right)
+
+    loop(gfeat.shape[0] // ROWS, enc_first)
+    when_all(has_south, g_north[3:], "wait_recv")
+    when_all(has_north, g_south[3:], "wait_recv")
     total[...] = jnp.zeros_like(total)
-    live = blocks[band, patch] * 128
+    live = blocks[patch, band] * 128
 
     def enc_edges(i):
-        before = pre_e[at(i)] + dot(pick(cols_g[at(i)], 4 * lon, 5 * lon), table[4:9].reshape(5 * lon, latent))
+        place = cols_g[at(i)]
+        left = jnp.concatenate([pick(place, n * lon, lon) for n in (5, 7)], axis=1)
+        right = jnp.concatenate([table[n].reshape(lon, latent) for n in (5, 7)], axis=0)
+        before = pre_e[at(i)] + dot(left, right)
         message = layer_norm(dot(silu(before).astype(BF), encw[3])).astype(BF)
         edge = lax.broadcasted_iota(jnp.int32, (1, ROWS), 1) + i * ROWS
         receiver = jnp.where(edge < live, grecv[:, at(i)], -1)
@@ -394,6 +422,7 @@
         return (current.astype(F32) + layer_norm(dot(hidden, weights[first + 2]))).astype(BF)
 
     mnext[...] = mesh_step(mesh[...], encw, 4)
+    sent(g_north, g_south, [g_west, g_east], g_north_on, g_south_on)
 
     pown[...] = dot(mnext[...], procw[0]).astype(BF)
     pcoarse[patch, band] = pown[nodes - COARSE_DEV :]
@@ -458,23 +487,33 @@
     loop(pfeat.shape[0] // ROWS - half, lambda i: proc_own(i + half))
     for _, in_copy in over:
         in_copy.wait_recv()
+    sides = 4 * BORDER
+    distant_rows = bands * patches * COARSE_DEV
+
+    def proc_first(i):
+        right = jnp.concatenate(
+            [pnear[0:4].reshape(sides, latent), pcoarse[...].reshape(distant_rows, latent)], axis=0
+        )
+        pre_e[at(i)] = pre_e[at(i)] + dot(pick(cols_p[at(i)], nodes, sides + distant_rows), right)
+
+    for copy in p_near[2]:
+        copy.wait_recv()
+    loop(pfeat.shape[0] // ROWS, proc_first)
+    arrived([], *p_near[3:])
+
+    total[...] = jnp.zeros_like(total)
+
+    def proc_edges(i):
+        corners = pick(cols_p[at(i)], nodes + sides + distant_rows, sides)
+        before = pre_e[at(i)] + dot(corners, pnear[4:8].reshape(sides, latent))
+        message = layer_norm(dot(silu(before).astype(BF), procw[3])).astype(BF)
+        total[...] += dot(scatter(precv[:, at(i)], nodes), message)
+
+    loop(pfeat.shape[0] // ROWS, proc_edges, 2)
+    last = mesh_step(mnext[...], procw, 4)
     for out_copy, _ in columns + across + over:
         out_copy.wait_send()
-    finish(*p_near)
-
-    total[...] = jnp.zeros_like(total)
-    far = 8 * BORDER + bands * patches * COARSE_DEV
-
-    def proc_edges(i):
-        right = jnp.concatenate(
-            [pnear[...].reshape(8 * BORDER, latent), pcoarse[...].reshape(far - 8 * BORDER, latent)], axis=0
-        )
-        before = pre_e[at(i)] + dot(pick(cols_p[at(i)], nodes, far), right)
-        message = layer_norm(dot(silu(before).astype(BF), procw[3])).astype(BF)
-        total[...] += dot(scatter(precv[:, at(i)], nodes), message)
-
-    loop(pfeat.shape[0] // ROWS, proc_edges, 2)
-    last = mesh_step(mnext[...], procw, 4)
+    sent(*p_near)
 
     down[...] = dot(last, decw[0]).astype(BF)
     d_near = near_copies(down, dnear, D_FIRST)
@@ -493,13 +532,22 @@
     for i in range(1, grid_steps):
         dec_own(i)
     pass_chunk(1, *d_near)
-    finish(*d_near)
+    for copy in d_near[2]:
+        copy.wait_recv()
+
+    def dec_first(i):
+        for k in range(3):
+            left = pick(cols_d[k, at(i)], nodes, sides)
+            pre_d[k, at(i)] = pre_d[k, at(i)] + dot(left, dnear[0:4].reshape(sides, latent))
+
+    loop(grid_steps, dec_first)
+    arrived([], *d_near[3:])
 
     def dec_edges(i):
-        near = dnear[...].reshape(8 * BORDER, latent)
+        near = dnear[4:8].reshape(sides, latent)
         summed = jnp.zeros((ROWS, latent), F32)
         for k in range(3):
-            before = pre_d[k, at(i)] + dot(pick(cols_d[k, at(i)], nodes, 8 * BORDER), near)
+            before = pre_d[k, at(i)] + dot(pick(cols_d[k, at(i)], nodes + sides, sides), near)
             message = layer_norm(dot(silu(before).astype(BF), decw[3])).astype(BF)
             summed = summed + message.astype(F32)
         hidden = silu(upd[at(i)] + dot(summed.astype(BF), decw[5])).astype(BF)
@@ -512,6 +560,7 @@
         part = pl.ds(i * half_lat, half_lat)
         stores.append(pltpu.make_async_copy(result.at[part], out.at[part], out_sem.at[i]))
         stores[-1].start()
+    sent(*d_near)
     for copy in stores:
         copy.wait()
 
@@ -556,7 +605,7 @@
                 vmem((edges, 128), jnp.int16),
                 vmem((pedges, 128), jnp.int16),
                 vmem((3, cells, 128), jnp.int16),
-                pltpu.SMEM((bands, patches), jnp.int32),
+                pltpu.SMEM((patches, bands), jnp.int32),
                 vmem((nodes, latent), F32),
                 vmem((nodes, latent), BF),
                 vmem((nodes, latent), BF),
@@ -576,7 +625,7 @@
                 collective_id=0, has_side_effects=True, vmem_limit_bytes=62 * 1024 * 1024
             ),
             cost_estimate=pl.CostEstimate(flops=24 * 10**9, bytes_accessed=24 * 10**6, transcendentals=5 * 10**6),
-        )(grid, mesh_state, gfeat, gsend, grecv, blocks, pfeat, psend, precv, dfeat, dsend, encw, procw, decw)
+        )(grid, mesh_state, gfeat, gsend, grecv, blocks.T, pfeat, psend, precv, dfeat, dsend, encw, procw, decw)
 
     placed = (
         P("band", "patch", None),

time: 74.1 us -> 70.9 us (0.957)
  Pallas kernels: 70.2 us -> 68.4 us
  local copies, waits for them, and re-layouts: 3.61 us -> 2.26 us
    pallas_call x1, Pallas kernels: 70.2 us -> 68.4 us  [shards(): pl.pallas_call(functools.partial(body, bands, patches), out_shape=jax.Sha...]
    unnamed x2 -> x1, local copies, waits for them, and re-layouts: 3.61 us -> 2.26 us
where the time goes in v3:
time: 70.9 us; the launch traced here: 70.7 us
  Pallas kernels  68.4 us (96%)
  local copies, waits for them, and re-layouts  2.26 us (3%)
    pallas_call x1, Pallas kernels, shards(): pl.pallas_call(functools.partial(body, bands, patches), out_shape=jax.Sha...  68.4 us
    unnamed x1, local copies, waits for them, and re-layouts  2.26 us

profile of v3, /device:TPU:9, one launch (start us, length us, event | category | flops | bytes accessed | tf_op | source)
XLA Modules:
  0.0 70.7 jit_solution(18053160055814896985)
XLA Ops:
  0.0 68.4 %shard_map.136 = bf16[4,256,512]{2,1,0:T(8,128)(2,1)} custom-call(bf16[4,256,512]{2,1,0:T(8,128)(2,1)} %grid_in.1, bf16[1,1,256,512]{3,2,1,0:T(8,128)(2,1)} %mesh_in.1, bf16[1,1,2048,512]{3,2,1,0:T(8,128)(2,1)} %gfeat_in.1, s32[1,1,2048]{2,1,0:T(1,128)} %gsend_in.1, s32[1,1,2048]{2,1,0:T(1,128)} %grecv_in.1, s32[4,8]{1,0:T(4,128)} %bitcast.1, ...), custom_call_target="tpu_custom_call" | custom-call | flops 24000000000 | bytes 24000000 | tf_op jit(solution)/shard_map/pallas_call | solution.py:579
  68.5 2.3 %copy.16 = bf16[4,256,512]{2,1,0:T(8,128)(2,1)} copy(bf16[4,256,512]{2,1,0:T(8,128)(2,1)} %shard_map.136) | data formatting | bytes 2097152

commit v4 on v3

--- a/solution.py
+++ b/solution.py
@@ -74,7 +74,8 @@
     encw_in,
     procw_in,
     decw_in,
-    out,
+    hidden_out,
+    gnext_out,
     grid,
     mesh,
     gfeat,
@@ -315,6 +316,8 @@
         gnext[at(i)] = (rows.astype(F32) + layer_norm(dot(hidden, encw[8]))).astype(BF)
 
     loop(grid_steps, self_step)
+    keep = pltpu.make_async_copy(gnext, gnext_out, out_sem.at[grid_steps])
+    keep.start()
     need("mesh", "e12")
     mrecv[...] = dot(mesh[...], encw[1]).astype(BF)
     need("e36")
@@ -375,18 +378,7 @@
 
     loop(pfeat.shape[0] // ROWS, proc_place)
 
-    def dec_place(i):
-        for k in range(3):
-            cols_d[k, at(i)] = dec_columns(k, i)
-
-    loop(grid_steps, dec_place)
-    need("d")
-
-    def dec_grid(i):
-        recv_d[at(i)] = dot(gnext[at(i)], decw[1]).astype(BF)
-
-    loop(grid_steps, dec_grid)
-    need("blocks", "p2", "pf", "p01", "df")
+    need("blocks", "p2", "pf", "p01", "d", "df")
 
     arrived([g_west, g_east], g_north_on, g_south_on)
     when_all(has_south, g_north[2:3], "wait_recv")
@@ -451,7 +443,9 @@
         pre_e[at(i)] = dot(left, right)
 
     def dec_update(i):
-        upd[at(i)] = dot(gnext[at(i)], decw[4])
+        both = dot(gnext[at(i)], jnp.concatenate([decw[1], decw[4]], axis=1))
+        recv_d[at(i)] = both[:, :latent].astype(BF)
+        upd[at(i)] = both[:, latent:]
 
     loop(grid_steps, dec_update)
 
@@ -523,6 +517,7 @@
         recv = recv_d[at(i)].astype(F32)
         right = jnp.concatenate([decw[2], down[...]], axis=0)
         for k in range(3):
+            cols_d[k, at(i)] = dec_columns(k, i)
             rows = dfeat[k, pl.ds(i * half_lat, half_lat)].reshape(ROWS, latent)
             left = jnp.concatenate([rows, pick(cols_d[k, at(i)], 0, nodes)], axis=1)
             pre_d[k, at(i)] = dot(left, right) + recv
@@ -551,18 +546,23 @@
             message = layer_norm(dot(silu(before).astype(BF), decw[3])).astype(BF)
             summed = summed + message.astype(F32)
         hidden = silu(upd[at(i)] + dot(summed.astype(BF), decw[5])).astype(BF)
-        rows = (gnext[at(i)].astype(F32) + layer_norm(dot(hidden, decw[6]))).astype(BF)
-        result[pl.ds(i * half_lat, half_lat)] = rows.reshape(half_lat, lon, latent)
+        result[at(i)] = hidden
 
     stores = []
     for i in range(grid_steps):
         dec_edges(i)
-        part = pl.ds(i * half_lat, half_lat)
-        stores.append(pltpu.make_async_copy(result.at[part], out.at[part], out_sem.at[i]))
+        part = pl.ds(i * ROWS, ROWS)
+        stores.append(pltpu.make_async_copy(result.at[part], hidden_out.at[part], out_sem.at[i]))
         stores[-1].start()
     sent(*d_near)
+    keep.wait()
     for copy in stores:
         copy.wait()
+
+
+def finish_body(hidden, current, weight, out):
+    rows = current[...].astype(F32) + layer_norm(dot(hidden[...], weight[0]))
+    out[0] = rows.astype(BF)
 
 
 def solution(mesh):
@@ -576,11 +576,11 @@
         any_spec = pl.BlockSpec(memory_space=pl.ANY)
         vmem = pltpu.VMEM
         copies = C_BASE + bands + patches
-        return pl.pallas_call(
+        hidden, current = pl.pallas_call(
             functools.partial(body, bands, patches),
-            out_shape=jax.ShapeDtypeStruct(grid.shape, BF),
+            out_shape=[jax.ShapeDtypeStruct((cells, latent), BF)] * 2,
             in_specs=[any_spec] * 14,
-            out_specs=any_spec,
+            out_specs=[any_spec] * 2,
             scratch_shapes=[
                 vmem(grid.shape, BF),
                 vmem((nodes, latent), BF),
@@ -615,9 +615,9 @@
                 vmem((cells, latent), BF),
                 vmem((nodes, latent), BF),
                 vmem((8, BORDER, latent), BF),
-                vmem(grid.shape, BF),
+                vmem((cells, latent), BF),
                 pltpu.SemaphoreType.DMA((19,)),
-                pltpu.SemaphoreType.DMA((2,)),
+                pltpu.SemaphoreType.DMA((cells // ROWS + 1,)),
                 pltpu.SemaphoreType.DMA((copies,)),
                 pltpu.SemaphoreType.DMA((copies,)),
             ],
@@ -626,6 +626,18 @@
             ),
             cost_estimate=pl.CostEstimate(flops=24 * 10**9, bytes_accessed=24 * 10**6, transcendentals=5 * 10**6),
         )(grid, mesh_state, gfeat, gsend, grecv, blocks.T, pfeat, psend, precv, dfeat, dsend, encw, procw, decw)
+        rows_spec = pl.BlockSpec((lon, latent), lambda i: (i, 0))
+        return pl.pallas_call(
+            finish_body,
+            grid=(lat,),
+            out_shape=jax.ShapeDtypeStruct(grid.shape, BF),
+            in_specs=[rows_spec, rows_spec, pl.BlockSpec((1, latent, latent), lambda i: (6, 0, 0))],
+            out_specs=pl.BlockSpec((1, lon, latent), lambda i: (i, 0, 0)),
+            compiler_params=pltpu.CompilerParams(vmem_limit_bytes=62 * 1024 * 1024),
+            cost_estimate=pl.CostEstimate(
+                flops=2 * cells * latent * latent, bytes_accessed=6 * cells * latent, transcendentals=cells
+            ),
+        )(hidden, current, decw)
 
     placed = (
         P("band", "patch", None),

time: 70.9 us -> 72.2 us (1.018)
  Pallas kernels: 68.4 us -> 72.1 us
  local copies, waits for them, and re-layouts: 2.26 us -> 0 us
    pallas_call x1 -> x2, Pallas kernels: 68.4 us -> 72.1 us  [the longest x1 67.4 us: shards(): pl.pallas_call(functools.partial(body, bands, patches), out_shape=[jax.Sh...]
    unnamed x1 -> x0, local copies, waits for them, and re-layouts: 2.26 us -> none
where the time goes in v4:
time: 72.2 us; the launch traced here: 72.1 us
  Pallas kernels  72.1 us (100%)
    pallas_call x1, Pallas kernels, shards(): pl.pallas_call(functools.partial(body, bands, patches), out_shape=[jax.Sh...  67.4 us
    pallas_call x1, Pallas kernels, shards(): pl.pallas_call(finish_body, grid=(lat,), out_shape=jax.ShapeDtypeStruct(g...  4.65 us

profile of v4, /device:TPU:9, one launch (start us, length us, event | category | flops | bytes accessed | tf_op | source)
XLA Modules:
  0.0 72.1 jit_solution(11849281807872723099)
XLA Ops:
  0.0 67.4 %shard_map.136 = (bf16[1024,512]{1,0:T(8,128)(2,1)}, bf16[1024,512]{1,0:T(8,128)(2,1)}) custom-call(bf16[4,256,512]{2,1,0:T(8,128)(2,1)} %grid_in.1, bf16[1,1,256,512]{3,2,1,0:T(8,128)(2,1)} %mesh_in.1, bf16[1,1,2048,512]{3,2,1,0:T(8,128)(2,1)} %gfeat_in.1, s32[1,1,2048]{2,1,0:T(1,128)} %gsend_in.1, s32[1,1,2048]{2,1,0:T(1,128)} %grecv_in.1, ...), custom_call_target="tpu_custom_call" | custom-call | flops 24000000000 | bytes 24000000 | tf_op jit(solution)/shard_map/pallas_call | solution.py:579
  67.4 4.6 %shard_map.137 = bf16[4,256,512]{2,1,0:T(8,128)(2,1)} custom-call(bf16[1024,512]{1,0:T(8,128)(2,1)} %get-tuple-element.7.hidden, bf16[1024,512]{1,0:T(8,128)(2,1)} %get-tuple-element.8.current, bf16[7,512,512]{2,1,0:T(8,128)(2,1)} %weight.1), custom_call_target="tpu_custom_call" | custom-call | flops 536870912 | bytes 3145728 | tf_op jit(solution)/shard_map/pallas_call | solution.py:630
